TPU v7x, 256 devices: a whole 4x4x8 slice. The times are simulated.
256 devices in a mesh: tile: 32 (over y, x, z_hi), lev: 8 (over z_lo, core).
Axes of the slice: x: 4, y: 4, z: 8 (z_hi: 2, z_lo: 4; z = z_hi * 4 + z_lo), core: 2. Of those that a mesh axis runs over, the one named last changes fastest.
Arguments:
- thickness: float32 [16, 256, 1024], P('lev', 'tile'), may hold values from 1 to 3
- wind_east: float32 [16, 256, 1024], P('lev', 'tile'), may hold values from -4 to 4
- wind_north: float32 [16, 256, 1024], P('lev', 'tile'), may hold values from -4 to 4
- theta: float32 [16, 256, 1024], P('lev', 'tile'), may hold values from 0.5 to 1.5
- tracer: float32 [16, 256, 1024], P('lev', 'tile'), may hold values from 0 to 1
- wind_vertical: float32 [16, 256, 1024], P('lev', 'tile'), may hold values from -2 to 2
- cross_index: int32 [15, 256, 1024], P(None, 'tile', 'lev'), may hold values from 0 to 15, as said below
- cross_slot: int32 [15, 256, 1024], P(None, 'tile', 'lev'), may hold values from 0 to 7, as said below
Outputs:
- remapped_thickness: float32 [16, 256, 1024], P(None, 'tile', 'lev')
- remapped_east: float32 [16, 256, 1024], P(None, 'tile', 'lev')
- remapped_north: float32 [16, 256, 1024], P(None, 'tile', 'lev')
- remapped_theta: float32 [16, 256, 1024], P(None, 'tile', 'lev')
- remapped_tracer: float32 [16, 256, 1024], P(None, 'tile', 'lev')
- remapped_vertical: float32 [16, 256, 1024], P(None, 'tile', 'lev')
Inputs may be any that keep to these rules, and one draw needn't show every extreme that they name: For each column the positions cross_index * 8 + cross_slot of interfaces j = 1 to 15 lie within 3 slots of j * 8, so they increase with j by 2 to 14 slots. `cross_slot`: slot within the layer named by cross_index, as described there.
All inputs are finite; a program needn't handle non-finite values.
Results may differ from a plain program's by a relative error of at most 0.000022.
Values sent between devices are 32-bit elements; how exact they have to be, the bound alone decides.
A program may use at most 64 MiB of HBM per device.

v0:
```python
import jax
import jax.numpy as jnp
from jax import lax
from jax.sharding import PartitionSpec as P

SUBSTEPS = 3
SLOTS = 8


courant = 0.1
damping = 0.015


def extended(cells, sides, width):
    for axis, dim in sides:
        count = lax.axis_size(axis)
        head = lax.slice_in_dim(cells, 0, width, axis=dim)
        tail = lax.slice_in_dim(cells, cells.shape[dim] - width, cells.shape[dim], axis=dim)
        cells = jnp.concatenate(
            [
                lax.ppermute(tail, axis, [(i, (i + 1) % count) for i in range(count)]),
                cells,
                lax.ppermute(head, axis, [((i + 1) % count, i) for i in range(count)]),
            ],
            axis=dim,
        )
    return cells


def strip(padded):
    length = padded.shape[-2]
    return padded[..., 3 : length - 3, :]


def along_x(padded):
    length = padded.shape[-2]

    def moved(offset):
        return padded[..., 3 + offset : length - 3 + offset, :]

    return (
        45.0 * (moved(1) - moved(-1)) - 9.0 * (moved(2) - moved(-2)) + (moved(3) - moved(-3))
    ) / 60.0


def sixth_x(padded):
    length = padded.shape[-2]

    def moved(offset):
        return padded[..., 3 + offset : length - 3 + offset, :]

    return (
        moved(3)
        + moved(-3)
        - 6.0 * (moved(2) + moved(-2))
        + 15.0 * (moved(1) + moved(-1))
        - 20.0 * moved(0)
    )


def wrap_y(field):
    return jnp.concatenate([field[..., -3:], field, field[..., :3]], axis=field.ndim - 1)


def y_slices(field):
    wrapped = wrap_y(field)
    width = field.shape[-1]

    def moved(offset):
        return wrapped[..., 3 + offset : 3 + offset + width]

    return moved


def along_y(field):
    moved = y_slices(field)
    return (
        45.0 * (moved(1) - moved(-1)) - 9.0 * (moved(2) - moved(-2)) + (moved(3) - moved(-3))
    ) / 60.0


def slope_sixth_y(field):
    moved = y_slices(field)
    first = (
        45.0 * (moved(1) - moved(-1)) - 9.0 * (moved(2) - moved(-2)) + (moved(3) - moved(-3))
    ) / 60.0
    second = (
        moved(3)
        + moved(-3)
        - 6.0 * (moved(2) + moved(-2))
        + 15.0 * (moved(1) + moved(-1))
        - 20.0 * moved(0)
    )
    return (first, second)


def advance(state):
    padded = extended(state, (("tile", 2),), 3)
    centre = strip(padded)
    slope_x = along_x(padded)
    slope_y, sixth_of_y = slope_sixth_y(centre)
    damps = damping * (sixth_x(padded) + sixth_of_y)
    east = centre[1]
    north = centre[2]
    divergence = slope_x[1] + slope_y[2]
    carried = east[None] * slope_x + north[None] * slope_y
    new_log = centre[0] - courant * (divergence + carried[0]) + damps[0]
    pressure = centre[3] * jnp.exp(new_log)
    press_pad = extended(pressure, (("tile", 1),), 3)
    press_x = along_x(press_pad)
    press_y = along_y(pressure)
    new_east = east - courant * (press_x + carried[1]) + damps[1]
    new_north = north - courant * (press_y + carried[2]) + damps[2]
    new_temper = centre[3] - courant * carried[3] + damps[3]
    new_mixing = centre[4] - courant * carried[4] + damps[4]
    new_upward = centre[5] - courant * (carried[5] + divergence) + damps[5]
    return jnp.stack([new_log, new_east, new_north, new_temper, new_mixing, new_upward], axis=0)


def layer_edges(field):
    inner = (7.0 * (field[1:-2] + field[2:-1]) - (field[:-3] + field[3:])) / 12.0
    return jnp.concatenate(
        [
            field[:1],
            0.5 * (field[:1] + field[1:2]),
            inner,
            0.5 * (field[-2:-1] + field[-1:]),
            field[-1:],
        ],
        axis=0,
    )


def running_before(weights):
    running = jnp.cumsum(weights, axis=0)
    before = jnp.concatenate([jnp.zeros_like(weights[:1]), running[:-1]], axis=0)
    return (before, running[-1:])


def select_layer(values, chooser):
    return jnp.sum(chooser * values[:, None], axis=0)


def remap_all(thick, fields, layer_index, fraction):
    levels = thick.shape[0]
    level_ids = lax.broadcasted_iota(jnp.int32, (levels, 1, 1, 1), 0)
    chooser = (layer_index[None] == level_ids).astype(jnp.float32)
    thick_at = select_layer(thick, chooser)
    mass_before, mass_total = running_before(thick)
    mass_cross = select_layer(mass_before, chooser) + fraction * thick_at
    mass_full = jnp.concatenate([jnp.zeros_like(mass_total), mass_cross, mass_total], axis=0)
    thickness_out = mass_full[1:] - mass_full[:-1]
    results = [thickness_out]
    square = 0.5 * fraction * fraction
    cubic = fraction * fraction * fraction / 3.0
    for field in fields:
        edges = layer_edges(field)
        left = edges[:-1]
        right = edges[1:]
        curve = 6.0 * field - 3.0 * (left + right)
        left_at = select_layer(left, chooser)
        right_at = select_layer(right, chooser)
        curve_at = select_layer(curve, chooser)
        partial_part = (
            fraction * left_at + square * (right_at - left_at) + curve_at * (square - cubic)
        )
        content_before, content_total = running_before(thick * field)
        cross = select_layer(content_before, chooser) + thick_at * partial_part
        full = jnp.concatenate([jnp.zeros_like(content_total), cross, content_total], axis=0)
        results.append((full[1:] - full[:-1]) / thickness_out)
    return results


def body(thickness, wind_east, wind_north, theta, tracer, wind_vertical, cross_index, cross_slot):
    state = jnp.stack(
        [jnp.log(thickness), wind_east, wind_north, theta, tracer, wind_vertical], axis=0
    )
    for step in range(SUBSTEPS):
        state = advance(state)
    state = jnp.concatenate([jnp.exp(state[:1]), state[1:]], axis=0)
    columns = lax.all_to_all(state, "lev", split_axis=3, concat_axis=1, tiled=True)
    fraction = cross_slot.astype(jnp.float32) / SLOTS
    results = remap_all(
        columns[0],
        [columns[1], columns[2], columns[3], columns[4], columns[5]],
        cross_index,
        fraction,
    )
    return (results[0], results[1], results[2], results[3], results[4], results[5])


def solution(mesh):
    placed = (
        P("lev", "tile", None),
        P("lev", "tile", None),
        P("lev", "tile", None),
        P("lev", "tile", None),
        P("lev", "tile", None),
        P("lev", "tile", None),
        P(None, "tile", "lev"),
        P(None, "tile", "lev"),
    )
    return jax.shard_map(
        body,
        mesh=mesh,
        in_specs=placed,
        out_specs=(
            P(None, "tile", "lev"),
            P(None, "tile", "lev"),
            P(None, "tile", "lev"),
            P(None, "tile", "lev"),
            P(None, "tile", "lev"),
            P(None, "tile", "lev"),
        ),
        check_vma=False,
    )
```

profile of v0, /device:TPU:1, one launch (start us, length us, event | category | flops | bytes accessed | tf_op | source)
XLA Modules:
  0.0 217.8 jit_solution(6509230739099343013)
XLA Ops:
  0.7 1.0 bitcast_dynamic-update-slice_fusion.18
  1.7 0.9 bitcast_dynamic-update-slice_fusion.17
  2.6 0.9 bitcast_dynamic-update-slice_fusion.16
  3.5 0.9 bitcast_dynamic-update-slice_fusion.15
  4.4 0.9 bitcast_dynamic-update-slice_fusion.14
  5.3 0.9 bitcast_dynamic-update-slice_fusion.13
  6.2 7.8 %collective-permute-start.1 = (f32[6,2,3,1024]{3,1,2,0:T(2,128)S(1)}, f32[6,2,3,1024]{3,1,2,0:T(2,128)S(1)}, u32[]{:S(2)}, u32[]{:S(2)}) collective-permute-start(f32[6,2,3,1024]{3,1,2,0:T(2,128)S(1)} %get-tuple-element.77), channel_id=1, source_target_pairs={{0,8},{8,16},{16,24},{24,32},{32,40},{40,48},{48,56},{56,64},{64,7... | collective-permute-start | bytes 442376 | tf_op jit(solution)/shard_map/ppermute | solution.py:21
  14.0 4.7 %collective-permute-start = (f32[6,2,3,1024]{3,1,2,0:T(2,128)S(1)}, f32[6,2,3,1024]{3,1,2,0:T(2,128)S(1)}, u32[]{:S(2)}, u32[]{:S(2)}) collective-permute-start(f32[6,2,3,1024]{3,1,2,0:T(2,128)S(1)} %get-tuple-element.78), channel_id=1, source_target_pairs={{8,0},{16,8},{24,16},{32,24},{40,32},{48,40},{56,48},{64,56},{72,6... | collective-permute-start | bytes 442376 | tf_op jit(solution)/shard_map/ppermute | solution.py:23
  18.7 1.0 copy_multiply_fusion
  19.9 2.3 %collective-permute-done.1 = f32[6,2,3,1024]{3,1,2,0:T(2,128)S(1)} collective-permute-done((f32[6,2,3,1024]{3,1,2,0:T(2,128)S(1)}, f32[6,2,3,1024]{3,1,2,0:T(2,128)S(1)}, u32[]{:S(2)}, u32[]{:S(2)}) %collective-permute-start.1) | collective-permute-done | bytes 147488 | tf_op jit(solution)/shard_map/ppermute | solution.py:21
  22.2 0.6 collective-permute-done
  22.7 3.5 %add_multiply_fusion.2 = f32[6,2,8,1024]{3,1,2,0:T(2,128)S(1)} fusion(f32[6,2,8,1024]{3,1,2,0:T(2,128)S(1)} %bitcast_dynamic-update-slice_fusion.13, f32[6,2,8,3]{3,1,2,0:T(2,128)S(1)} %get-tuple-element.80, f32[6,2,8,3]{3,1,2,0:T(2,128)S(1)} %get-tuple-element.79, f32[6,2,3,1024]{3,1,2,0:T(2,128)S(1)} %collective-permute-done, ...), kind=kLoop, calls=%fused_computation.103 | loop fusion | flops 3047424 | bytes 1083648 | tf_op jit(solution)/shard_map/mul | solution.py:102
  26.2 4.3 %multiply_add_fusion.2 = (f32[6,2,8,1024]{3,1,2,0:T(2,128)S(1)}, f32[6,2,8,1024]{3,1,2,0:T(2,128)S(1)}, f32[6,2,8,1024]{3,1,2,0:T(2,128)S(1)}) fusion(f32[2,8,1024]{2,0,1:T(2,128)S(1)} %get-tuple-element.137, f32[2,8,1024]{2,0,1:T(2,128)S(1)} %get-tuple-element.138, f32[6,2,8,1024]{3,1,2,0:T(2,128)S(1)} %bitcast_dynamic-update-slice_fusion.13, ...), kind=kLoop, calls=%fused_computation.104 | loop fusion | flops 2850816 | bytes 2001152 | tf_op jit(solution)/shard_map/add | solution.py:106
  30.5 1.1 exponential_multiply_fusion.1
  31.7 12.6 %collective-permute-start.2 = (f32[2,3,1024]{2,0,1:T(2,128)S(1)}, f32[2,3,1024]{2,0,1:T(2,128)S(1)}, u32[]{:S(2)}, u32[]{:S(2)}) collective-permute-start(f32[2,3,1024]{2,0,1:T(2,128)S(1)} %get-tuple-element.135), channel_id=1, source_target_pairs={{8,0},{16,8},{24,16},{32,24},{40,32},{48,40},{56,48},{64,56},{72,6... | collective-permute-start | bytes 73736 | tf_op jit(solution)/shard_map/ppermute | solution.py:23
  44.4 1.4 broadcast_multiply_fusion.2
  45.8 9.5 %collective-permute-done.3 = f32[2,3,1024]{2,0,1:T(2,128)S(1)} collective-permute-done((f32[2,3,1024]{2,0,1:T(2,128)S(1)}, f32[2,3,1024]{2,0,1:T(2,128)S(1)}, u32[]{:S(2)}, u32[]{:S(2)}) %collective-permute-start.3) | collective-permute-done | bytes 24608 | tf_op jit(solution)/shard_map/ppermute | solution.py:21
  55.2 0.2 broadcast_multiply_fusion.3
  55.7 0.2 bitcast_dynamic-update-slice_fusion.7
  56.0 9.6 %collective-permute-start.4 = (f32[6,2,3,1024]{3,1,2,0:T(2,128)S(1)}, f32[6,2,3,1024]{3,1,2,0:T(2,128)S(1)}, u32[]{:S(2)}, u32[]{:S(2)}) collective-permute-start(f32[6,2,3,1024]{3,1,2,0:T(2,128)S(1)} %get-tuple-element.74), channel_id=1, source_target_pairs={{8,0},{16,8},{24,16},{32,24},{40,32},{48,40},{56,48},{64,56},{72,6... | collective-permute-start | bytes 442376 | tf_op jit(solution)/shard_map/ppermute | solution.py:23
  65.7 5.0 %collective-permute-done.5 = f32[6,2,3,1024]{3,1,2,0:T(2,128)S(1)} collective-permute-done((f32[6,2,3,1024]{3,1,2,0:T(2,128)S(1)}, f32[6,2,3,1024]{3,1,2,0:T(2,128)S(1)}, u32[]{:S(2)}, u32[]{:S(2)}) %collective-permute-start.5) | collective-permute-done | bytes 147488 | tf_op jit(solution)/shard_map/ppermute | solution.py:21
  70.7 3.5 %add_multiply_fusion.1 = f32[6,2,8,1024]{3,1,2,0:T(2,128)S(1)} fusion(f32[6,2,8,1024]{3,1,2,0:T(2,128)S(1)} %get-tuple-element.52, f32[6,2,8,3]{3,1,2,0:T(2,128)S(1)} %get-tuple-element.76, f32[6,2,8,3]{3,1,2,0:T(2,128)S(1)} %get-tuple-element.75, f32[6,2,3,1024]{3,1,2,0:T(2,128)S(1)} %collective-permute-done.4, f32[6,2,3,1024]{3,1,2,0:T(2,128)S(1)} %collective-permute-done.5), kind=kLoop, calls=%fused_computation.99 | loop fusion | flops 3047424 | bytes 1083648 | tf_op jit(solution)/shard_map/mul | solution.py:102
  74.2 4.3 %multiply_add_fusion.1 = (f32[6,2,8,1024]{3,1,2,0:T(2,128)S(1)}, f32[6,2,8,1024]{3,1,2,0:T(2,128)S(1)}, f32[6,2,8,1024]{3,1,2,0:T(2,128)S(1)}) fusion(f32[2,8,1024]{2,0,1:T(2,128)S(1)} %get-tuple-element.50, f32[2,8,1024]{2,0,1:T(2,128)S(1)} %get-tuple-element.48, f32[6,2,8,1024]{3,1,2,0:T(2,128)S(1)} %get-tuple-element.52, ...), kind=kLoop, calls=%fused_computation.100 | loop fusion | flops 2850816 | bytes 2001152 | tf_op jit(solution)/shard_map/add | solution.py:106
  78.5 0.1 exponential_multiply_fusion
  78.7 7.6 %collective-permute-start.6 = (f32[2,3,1024]{2,0,1:T(2,128)S(1)}, f32[2,3,1024]{2,0,1:T(2,128)S(1)}, u32[]{:S(2)}, u32[]{:S(2)}) collective-permute-start(f32[2,3,1024]{2,0,1:T(2,128)S(1)} %get-tuple-element.131), channel_id=1, source_target_pairs={{8,0},{16,8},{24,16},{32,24},{40,32},{48,40},{56,48},{64,56},{72,6... | collective-permute-start | bytes 73736 | tf_op jit(solution)/shard_map/ppermute | solution.py:23
  86.3 0.5 broadcast_multiply_fusion
  86.8 0.4 collective-permute-done.6
  87.2 9.9 %collective-permute-done.7 = f32[2,3,1024]{2,0,1:T(2,128)S(1)} collective-permute-done((f32[2,3,1024]{2,0,1:T(2,128)S(1)}, f32[2,3,1024]{2,0,1:T(2,128)S(1)}, u32[]{:S(2)}, u32[]{:S(2)}) %collective-permute-start.7) | collective-permute-done | bytes 24608 | tf_op jit(solution)/shard_map/ppermute | solution.py:21
  97.7 9.6 %collective-permute-start.8 = (f32[6,2,3,1024]{3,1,2,0:T(2,128)S(1)}, f32[6,2,3,1024]{3,1,2,0:T(2,128)S(1)}, u32[]{:S(2)}, u32[]{:S(2)}) collective-permute-start(f32[6,2,3,1024]{3,1,2,0:T(2,128)S(1)} %get-tuple-element.70), channel_id=1, source_target_pairs={{8,0},{16,8},{24,16},{32,24},{40,32},{48,40},{56,48},{64,56},{72,6... | collective-permute-start | bytes 442376 | tf_op jit(solution)/shard_map/ppermute | solution.py:23
  107.4 4.3 %collective-permute-done.9 = f32[6,2,3,1024]{3,1,2,0:T(2,128)S(1)} collective-permute-done((f32[6,2,3,1024]{3,1,2,0:T(2,128)S(1)}, f32[6,2,3,1024]{3,1,2,0:T(2,128)S(1)}, u32[]{:S(2)}, u32[]{:S(2)}) %collective-permute-start.9) | collective-permute-done | bytes 147488 | tf_op jit(solution)/shard_map/ppermute | solution.py:21
  111.7 3.5 %add_multiply_fusion = f32[6,2,8,1024]{3,1,2,0:T(2,128)S(1)} fusion(f32[6,2,8,1024]{3,1,2,0:T(2,128)S(1)} %get-tuple-element.39, f32[6,2,8,3]{3,1,2,0:T(2,128)S(1)} %get-tuple-element.72, f32[6,2,8,3]{3,1,2,0:T(2,128)S(1)} %get-tuple-element.71, f32[6,2,3,1024]{3,1,2,0:T(2,128)S(1)} %collective-permute-done.8, f32[6,2,3,1024]{3,1,2,0:T(2,128)S(1)} %collective-permute-done.9), kind=kLoop, calls=%fused_computation.95 | loop fusion | flops 3047424 | bytes 1083648 | tf_op jit(solution)/shard_map/mul | solution.py:102
  115.2 4.3 %multiply_add_fusion = (f32[6,2,8,1024]{3,1,2,0:T(2,128)S(1)}, f32[6,2,8,1024]{3,1,2,0:T(2,128)S(1)}, f32[6,2,8,1024]{3,1,2,0:T(2,128)S(1)}) fusion(f32[2,8,1024]{2,0,1:T(2,128)S(1)} %get-tuple-element.37, f32[2,8,1024]{2,0,1:T(2,128)S(1)} %get-tuple-element.35, f32[6,2,8,1024]{3,1,2,0:T(2,128)S(1)} %get-tuple-element.39, ...), kind=kLoop, calls=%fused_computation.96 | loop fusion | flops 2850816 | bytes 2001152 | tf_op jit(solution)/shard_map/add | solution.py:106
  119.7 8.7 %collective-permute-start.10 = (f32[2,3,1024]{2,0,1:T(2,128)S(1)}, f32[2,3,1024]{2,0,1:T(2,128)S(1)}, u32[]{:S(2)}, u32[]{:S(2)}) collective-permute-start(f32[2,3,1024]{2,0,1:T(2,128)S(1)} %get-tuple-element.127), channel_id=1, source_target_pairs={{8,0},{16,8},{24,16},{32,24},{40,32},{48,40},{56,48},{64,56},{72,6... | collective-permute-start | bytes 73736 | tf_op jit(solution)/shard_map/ppermute | solution.py:23
  128.5 0.9 collective-permute-done.10
  129.3 9.9 %collective-permute-done.11 = f32[2,3,1024]{2,0,1:T(2,128)S(1)} collective-permute-done((f32[2,3,1024]{2,0,1:T(2,128)S(1)}, f32[2,3,1024]{2,0,1:T(2,128)S(1)}, u32[]{:S(2)}, u32[]{:S(2)}) %collective-permute-start.11) | collective-permute-done | bytes 24608 | tf_op jit(solution)/shard_map/ppermute | solution.py:21
  139.3 0.5 fusion.90
  140.2 6.6 %copy.212 = f32[6,2,8,1024]{2,1,0,3:T(2,128)} copy(f32[6,2,8,1024]{3,1,2,0:T(2,128)S(1)} %fusion.74) | data formatting | bytes 786432 | tf_op jit(solution)/shard_map/concatenate | solution.py:180
  146.8 10.2 %reshape.403 = f32[8,1,12288]{2,1,0:T(1,128)S(1)} reshape(f32[1024,6,2,8]{3,2,1,0:T(2,128)} %bitcast.334) | data formatting | bytes 786432
  157.0 25.2 %all_to_all.15 = f32[8,1,12288]{2,1,0:T(1,128)S(1)} all-to-all(f32[8,1,12288]{2,1,0:T(1,128)S(1)} %reshape.403), channel_id=1, replica_groups=mesh['tile'=32,'lev'=8] {'lev'}, dimensions={0} | all-to-all | bytes 786432 | tf_op jit(solution)/shard_map/all_to_all | solution.py:181
  182.2 0.5 broadcast.385
  182.8 1.6 reduce
  184.3 12.3 %reshape.404 = f32[1024,6,2,8]{3,2,1,0:T(2,128)} reshape(f32[8,12288]{1,0:T(8,128)S(1)} %reduce) | data formatting | bytes 786432
  196.6 4.0 %fusion.219 = (f32[1,8,2,8,128]{3,2,0,4,1:T(2,128)}, f32[1,8,2,8,128]{3,2,0,4,1:T(2,128)}, f32[1,8,2,8,128]{3,2,0,4,1:T(2,128)}, f32[1,8,2,8,128]{3,2,0,4,1:T(2,...) fusion(f32[6,8,2,8,128]{3,2,0,4,1:T(2,128)} %bitcast.333), kind=kLoop, calls=%fused_computation.458 | loop fusion | bytes 786432 | tf_op jit(solution)/shard_map/slice | solution.py:185
  200.6 1.4 copy.214
  202.0 0.6 fusion.226
  202.6 0.6 fusion.194
  203.3 1.4 copy.218
  204.6 0.7 fusion.182
  205.3 1.4 copy.217
  206.6 0.6 fusion.229
  207.3 0.6 fusion.185
  207.9 0.4 copy.216
  208.4 0.4 copy.215
  208.8 0.4 copy.213
  209.5 0.7 fusion.237
  210.3 0.9 pad_maximum_fusion.24
  211.2 0.3 select_reduce_fusion.18
  211.6 0.9 pad_maximum_fusion.30
  212.5 0.9 pad_maximum_fusion.33
  213.4 1.2 select_reduce_fusion.2
  214.6 0.9 multiply_add_fusion.7
  215.5 1.0 multiply_add_fusion.4
  216.5 0.6 fusion.168
  217.1 0.7 fusion.167
  (82 shorter events, 2.5 us)
Async XLA Ops:
  0.6 54.6 %copy-start = (f32[2,8,1024]{2,1,0:T(8,128)S(1)}, f32[2,8,1024]{2,1,0:T(8,128)}, u32[]{:S(2)}) copy-start(f32[2,8,1024]{2,1,0:T(8,128)} %param.9) | copy-start | bytes 196612
  0.6 54.8 %copy-start.1 = (f32[2,8,1024]{2,1,0:T(8,128)S(1)}, f32[2,8,1024]{2,1,0:T(8,128)}, u32[]{:S(2)}) copy-start(f32[2,8,1024]{2,1,0:T(8,128)} %param.11) | copy-start | bytes 196612
  0.7 54.9 %copy-start.2 = (f32[2,8,1024]{2,1,0:T(8,128)S(1)}, f32[2,8,1024]{2,1,0:T(8,128)}, u32[]{:S(2)}) copy-start(f32[2,8,1024]{2,1,0:T(8,128)} %param.12) | copy-start | bytes 196612
  0.7 55.0 %copy-start.3 = (f32[2,8,1024]{2,1,0:T(8,128)S(1)}, f32[2,8,1024]{2,1,0:T(8,128)}, u32[]{:S(2)}) copy-start(f32[2,8,1024]{2,1,0:T(8,128)} %param.13) | copy-start | bytes 196612
  6.2 16.0 %collective-permute-start.1 = (f32[6,2,3,1024]{3,1,2,0:T(2,128)S(1)}, f32[6,2,3,1024]{3,1,2,0:T(2,128)S(1)}, u32[]{:S(2)}, u32[]{:S(2)}) collective-permute-start(f32[6,2,3,1024]{3,1,2,0:T(2,128)S(1)} %get-tuple-element.77), channel_id=1, source_target_pairs={{0,8},{8,16},{16,24},{24,32},{32,40},{40,48},{48,56},{56,64},{64,7... | collective-permute-start | bytes 442376 | tf_op jit(solution)/shard_map/ppermute | solution.py:21
  14.0 8.7 %collective-permute-start = (f32[6,2,3,1024]{3,1,2,0:T(2,128)S(1)}, f32[6,2,3,1024]{3,1,2,0:T(2,128)S(1)}, u32[]{:S(2)}, u32[]{:S(2)}) collective-permute-start(f32[6,2,3,1024]{3,1,2,0:T(2,128)S(1)} %get-tuple-element.78), channel_id=1, source_target_pairs={{8,0},{16,8},{24,16},{32,24},{40,32},{48,40},{56,48},{64,56},{72,6... | collective-permute-start | bytes 442376 | tf_op jit(solution)/shard_map/ppermute | solution.py:23
  31.7 14.0 %collective-permute-start.2 = (f32[2,3,1024]{2,0,1:T(2,128)S(1)}, f32[2,3,1024]{2,0,1:T(2,128)S(1)}, u32[]{:S(2)}, u32[]{:S(2)}) collective-permute-start(f32[2,3,1024]{2,0,1:T(2,128)S(1)} %get-tuple-element.135), channel_id=1, source_target_pairs={{8,0},{16,8},{24,16},{32,24},{40,32},{48,40},{56,48},{64,56},{72,6... | collective-permute-start | bytes 73736 | tf_op jit(solution)/shard_map/ppermute | solution.py:23
  44.4 10.9 %collective-permute-start.3 = (f32[2,3,1024]{2,0,1:T(2,128)S(1)}, f32[2,3,1024]{2,0,1:T(2,128)S(1)}, u32[]{:S(2)}, u32[]{:S(2)}) collective-permute-start(f32[2,3,1024]{2,0,1:T(2,128)S(1)} %get-tuple-element.136), channel_id=1, source_target_pairs={{0,8},{8,16},{16,24},{24,32},{32,40},{40,48},{48,56},{56,64},{64,7... | collective-permute-start | bytes 73736 | tf_op jit(solution)/shard_map/ppermute | solution.py:21
  55.9 14.8 %collective-permute-start.5 = (f32[6,2,3,1024]{3,1,2,0:T(2,128)S(1)}, f32[6,2,3,1024]{3,1,2,0:T(2,128)S(1)}, u32[]{:S(2)}, u32[]{:S(2)}) collective-permute-start(f32[6,2,3,1024]{3,1,2,0:T(2,128)S(1)} %get-tuple-element.73), channel_id=1, source_target_pairs={{0,8},{8,16},{16,24},{24,32},{32,40},{40,48},{48,56},{56,64},{64,7... | collective-permute-start | bytes 442376 | tf_op jit(solution)/shard_map/ppermute | solution.py:21
  56.0 14.7 %collective-permute-start.4 = (f32[6,2,3,1024]{3,1,2,0:T(2,128)S(1)}, f32[6,2,3,1024]{3,1,2,0:T(2,128)S(1)}, u32[]{:S(2)}, u32[]{:S(2)}) collective-permute-start(f32[6,2,3,1024]{3,1,2,0:T(2,128)S(1)} %get-tuple-element.74), channel_id=1, source_target_pairs={{8,0},{16,8},{24,16},{32,24},{40,32},{48,40},{56,48},{64,56},{72,6... | collective-permute-start | bytes 442376 | tf_op jit(solution)/shard_map/ppermute | solution.py:23
  78.7 8.5 %collective-permute-start.6 = (f32[2,3,1024]{2,0,1:T(2,128)S(1)}, f32[2,3,1024]{2,0,1:T(2,128)S(1)}, u32[]{:S(2)}, u32[]{:S(2)}) collective-permute-start(f32[2,3,1024]{2,0,1:T(2,128)S(1)} %get-tuple-element.131), channel_id=1, source_target_pairs={{8,0},{16,8},{24,16},{32,24},{40,32},{48,40},{56,48},{64,56},{72,6... | collective-permute-start | bytes 73736 | tf_op jit(solution)/shard_map/ppermute | solution.py:23
  86.3 10.8 %collective-permute-start.7 = (f32[2,3,1024]{2,0,1:T(2,128)S(1)}, f32[2,3,1024]{2,0,1:T(2,128)S(1)}, u32[]{:S(2)}, u32[]{:S(2)}) collective-permute-start(f32[2,3,1024]{2,0,1:T(2,128)S(1)} %get-tuple-element.132), channel_id=1, source_target_pairs={{0,8},{8,16},{16,24},{24,32},{32,40},{40,48},{48,56},{56,64},{64,7... | collective-permute-start | bytes 73736 | tf_op jit(solution)/shard_map/ppermute | solution.py:21
  97.6 14.1 %collective-permute-start.9 = (f32[6,2,3,1024]{3,1,2,0:T(2,128)S(1)}, f32[6,2,3,1024]{3,1,2,0:T(2,128)S(1)}, u32[]{:S(2)}, u32[]{:S(2)}) collective-permute-start(f32[6,2,3,1024]{3,1,2,0:T(2,128)S(1)} %get-tuple-element.69), channel_id=1, source_target_pairs={{0,8},{8,16},{16,24},{24,32},{32,40},{40,48},{48,56},{56,64},{64,7... | collective-permute-start | bytes 442376 | tf_op jit(solution)/shard_map/ppermute | solution.py:21
  97.7 14.0 %collective-permute-start.8 = (f32[6,2,3,1024]{3,1,2,0:T(2,128)S(1)}, f32[6,2,3,1024]{3,1,2,0:T(2,128)S(1)}, u32[]{:S(2)}, u32[]{:S(2)}) collective-permute-start(f32[6,2,3,1024]{3,1,2,0:T(2,128)S(1)} %get-tuple-element.70), channel_id=1, source_target_pairs={{8,0},{16,8},{24,16},{32,24},{40,32},{48,40},{56,48},{64,56},{72,6... | collective-permute-start | bytes 442376 | tf_op jit(solution)/shard_map/ppermute | solution.py:23
  119.7 9.6 %collective-permute-start.10 = (f32[2,3,1024]{2,0,1:T(2,128)S(1)}, f32[2,3,1024]{2,0,1:T(2,128)S(1)}, u32[]{:S(2)}, u32[]{:S(2)}) collective-permute-start(f32[2,3,1024]{2,0,1:T(2,128)S(1)} %get-tuple-element.127), channel_id=1, source_target_pairs={{8,0},{16,8},{24,16},{32,24},{40,32},{48,40},{56,48},{64,56},{72,6... | collective-permute-start | bytes 73736 | tf_op jit(solution)/shard_map/ppermute | solution.py:23
  128.4 10.8 %collective-permute-start.11 = (f32[2,3,1024]{2,0,1:T(2,128)S(1)}, f32[2,3,1024]{2,0,1:T(2,128)S(1)}, u32[]{:S(2)}, u32[]{:S(2)}) collective-permute-start(f32[2,3,1024]{2,0,1:T(2,128)S(1)} %get-tuple-element.128), channel_id=1, source_target_pairs={{0,8},{8,16},{16,24},{24,32},{32,40},{40,48},{48,56},{56,64},{64,7... | collective-permute-start | bytes 73736 | tf_op jit(solution)/shard_map/ppermute | solution.py:21
  200.6 10.5 %copy-start.5 = (s32[15,8,128]{2,1,0:T(8,128)S(1)}, s32[15,8,128]{2,1,0:T(8,128)}, u32[]{:S(2)}) copy-start(s32[15,8,128]{2,1,0:T(8,128)} %param.14) | copy-start | bytes 184324
  208.3 3.2 %copy-start.6 = (f32[1,8,128]{2,1,0:T(8,128)S(1)}, f32[1,8,128]{2,1,0:T(8,128)}, u32[]{:S(2)}) copy-start(f32[1,8,128]{2,1,0:T(8,128)} %get-tuple-element.115) | copy-start | bytes 12292
  217.1 0.7 copy-start.4
where the time goes:
time: 219 us; the launch traced here: 218 us
  starting transfers between devices  60.8 us (28%)
  local copies, waits for them, and re-layouts  45.2 us (21%)
  other arithmetic  42.8 us (20%)
  waiting for transfers between devices  42.7 us (19%)
  blocking collectives  25.2 us (12%)
    ppermute x6, starting transfers between devices, extended(): lax.ppermute(head, axis, [((i + 1) % count, i) for i in range(count)])  52.8 us
    ppermute x6, waiting for transfers between devices, extended(): lax.ppermute(tail, axis, [(i, (i + 1) % count) for i in range(count)])  40.8 us
    unnamed x28, local copies, waits for them, and re-layouts  27.2 us
    all_to_all x1, blocking collectives, body(): lax.all_to_all(state, 'lev', split_axis=3, concat_axis=1, tiled=True)  25.2 us
    add x3, other arithmetic, advance(): carried = east[None] * slope_x + north[None] * slope_y  12.9 us
    mul x3, other arithmetic, advance(): damps = damping * (sixth_x(padded) + sixth_of_y)  10.5 us
    ppermute x6, starting transfers between devices, extended(): lax.ppermute(tail, axis, [(i, (i + 1) % count) for i in range(count)])  7.99 us
    concatenate x1, local copies, waits for them, and re-layouts, body(): state = jnp.concatenate([jnp.exp(state[:1]), state[1:]], axis=0)  6.61 us
  transfers between devices with their start and end apart: 12, of which 9 were waited for; matrix products, arithmetic and copies ran while one was open for 2% of the time, Pallas kernels for 0%

commit v1 on v0

v1 whole, which is shorter than its diff:
```python
import functools

import jax
import jax.numpy as jnp
from jax import lax
from jax.experimental import pallas as pl
from jax.experimental.pallas import tpu as pltpu
from jax.sharding import PartitionSpec as P

MESH = pl.DeviceIdType.MESH

COURANT = 0.1
DAMPING = 0.015
SLOPE = (45.0 / 60.0, -9.0 / 60.0, 1.0 / 60.0)
SIXTH = (15.0, -6.0, 1.0)
SLOTS = 8

LANES = 128
SUB = 8
PIECES = 8
LEVELS = 16
FIELDS = 6
COLUMNS = 16
OFF = 24
ROWS = 64

REACH = (((0, 16), (0, 16)), ((0, 16), (0, 16)), ((1, 15), (0, 15)), ((1, 15), (0, 15)), ((7, 9), (0, 9)), ((7, 9), (0, 9)))


def place():
    tile = lax.axis_index("tile")
    lev = lax.axis_index("lev")
    high = lax.rem(tile, 2)
    column = lax.div(tile, 2)
    ring = high * 4 + lax.div(lev, 2)
    core = lax.rem(lev, 2)
    return column, ring, core


def device(column, ring, core):
    column = lax.rem(column + 2 * COLUMNS, COLUMNS)
    ring = lax.rem(ring + 16, 8)
    return (column * 2 + lax.div(ring, 4), lax.rem(ring, 4) * 2 + core)


def owned_level(ring, core):
    first = jnp.logical_and(ring >= 2, ring < 6)
    early = 4 * (ring - 2) + 2 * core
    late = 4 * lax.rem(ring + 2, 8) + 2 * core + 1
    return jnp.where(first, early, late)


def lanes():
    return lax.broadcasted_iota(jnp.int32, (SUB, LANES), 1)


def shifted_y(get, piece, row, lane):
    before = lax.rem(piece + PIECES - 1, PIECES)
    after = lax.rem(piece + 1, PIECES)
    here, left, right = get(piece, row), get(before, row), get(after, row)
    ahead, behind = [], []
    for k in (1, 2, 3):
        ahead.append(pltpu.roll(jnp.where(lane < k, right, here), LANES - k, 1))
        behind.append(pltpu.roll(jnp.where(lane >= LANES - k, left, here), k, 1))
    return here, ahead, behind


def shifted_x(get, piece, row):
    return [get(piece, row + k) for k in (1, 2, 3)], [get(piece, row - k) for k in (1, 2, 3)]


def slope(ahead, behind):
    total = None
    for k in range(3):
        term = (-COURANT * SLOPE[k]) * (ahead[k] - behind[k])
        total = term if total is None else total + term
    return total


def weights(wind):
    plus, minus = [], []
    for k in range(3):
        carry = wind * (-COURANT * SLOPE[k])
        plus.append(DAMPING * SIXTH[k] + carry)
        minus.append(DAMPING * SIXTH[k] - carry)
    return plus, minus


def stencil(here, x_side, y_side, by_x, by_y):
    total = (1.0 - 40.0 * DAMPING) * here
    for (ahead, behind), (plus, minus) in ((x_side, by_x), (y_side, by_y)):
        for k in range(3):
            total = total + plus[k] * ahead[k]
            total = total + minus[k] * behind[k]
    return total


def reader(ref, field):
    def get(piece, row):
        return ref[field, piece, pl.ds(OFF + row, SUB), :]

    return get


def mass_stage(log_get, old, pressure, divergence, step, start, blocks, store):
    def run(piece, carry):
        lane = lanes()
        for block in range(blocks):
            row = start + SUB * block
            east = reader(old, 1)
            north = reader(old, 2)
            by_x = weights(east(piece, row))
            n_here, n_ahead, n_behind = shifted_y(north, piece, row, lane)
            by_y = weights(n_here)
            div = slope(*shifted_x(east, piece, row)) + slope(n_ahead, n_behind)
            g_here, g_ahead, g_behind = shifted_y(log_get, piece, row, lane)
            new = stencil(g_here, shifted_x(log_get, piece, row), (g_ahead, g_behind), by_x, by_y) + div
            thick = jnp.exp(new)
            at = pl.ds(OFF + row, SUB)
            divergence[step, piece, at, :] = div
            pressure[step, piece, at, :] = reader(old, 3)(piece, row) * thick
            store(piece, row, new, thick)
        return carry

    lax.fori_loop(0, PIECES, run, 0)


def wind_piece(old, pressure, step, piece, row, lane):
    east, north, temper, press = reader(old, 1), reader(old, 2), reader(old, 3), reader(pressure, step)
    e_here, e_ahead, e_behind = shifted_y(east, piece, row, lane)
    n_here, n_ahead, n_behind = shifted_y(north, piece, row, lane)
    by_x, by_y = weights(e_here), weights(n_here)
    new_east = stencil(e_here, shifted_x(east, piece, row), (e_ahead, e_behind), by_x, by_y)
    new_east = new_east + slope(*shifted_x(press, piece, row))
    new_north = stencil(n_here, shifted_x(north, piece, row), (n_ahead, n_behind), by_x, by_y)
    _, p_ahead, p_behind = shifted_y(press, piece, row, lane)
    new_north = new_north + slope(p_ahead, p_behind)
    t_here, t_ahead, t_behind = shifted_y(temper, piece, row, lane)
    new_temper = stencil(t_here, shifted_x(temper, piece, row), (t_ahead, t_behind), by_x, by_y)
    return new_east, new_north, new_temper


def passive_piece(old, divergence, step, piece, row, lane):
    by_x = weights(reader(old, 1)(piece, row))
    by_y = weights(reader(old, 2)(piece, row))
    out = []
    for field in (4, 5):
        get = reader(old, field)
        here, ahead, behind = shifted_y(get, piece, row, lane)
        out.append(stencil(here, shifted_x(get, piece, row), (ahead, behind), by_x, by_y))
    out[1] = out[1] + divergence[step, piece, pl.ds(OFF + row, SUB), :]
    return out


def stage(body, start, blocks, store):
    def run(piece, carry):
        lane = lanes()
        for block in range(blocks):
            row = start + SUB * block
            store(piece, row, body(piece, row, lane))
        return carry

    lax.fori_loop(0, PIECES, run, 0)


def advance_kernel(*refs):
    inputs = refs[:FIELDS]
    got_a, got_b = refs[FIELDS : FIELDS + 2]
    (state0, state1, state2, logs, pressure, divergence, out_a, out_b, z_send, z_recv, x_send, x_recv, far_send, far_recv, all_send, all_recv, own_sem) = refs[FIELDS + 2 :]

    column, ring, core = place()
    high = lax.div(ring, 4)

    barrier = pltpu.get_barrier_semaphore()
    partners = [device(column + d, ring, core) for d in (1, -1, 2, -2)]
    partners += [device(column, ring + d, lax.rem(core + c, 2)) for d in (4, 3, 5, 2, 6, 1, 7, 0) for c in (0, 1) if d or c]
    for who in partners:
        pl.semaphore_signal(barrier, inc=1, device_id=who, device_id_type=MESH)
    pl.semaphore_wait(barrier, len(partners))

    half = pl.ds(pl.multiple_of(OFF + SUB * high, SUB), SUB)
    sends = []
    z_copies = []
    for field in range(FIELDS):
        pair = []
        for way, (level, hop) in enumerate(((high, 2), (1 - high, -2))):
            copy = pltpu.make_async_remote_copy(
                src_ref=inputs[field].at[level],
                dst_ref=state0.at[field, :, half, :],
                send_sem=z_send.at[field, way],
                recv_sem=z_recv.at[field, way],
                device_id=device(column, ring + hop, core),
                device_id_type=MESH,
            )
            copy.start()
            pair.append(copy)
            sends.append(copy)
        z_copies.append(pair)

    x_copies = []
    for field in range(FIELDS):
        for copy in z_copies[field]:
            copy.wait_recv()
        group = []
        for way in (0, 1):
            first, count = REACH[field][way]
            shift = -16 if way == 0 else 16
            copy = pltpu.make_async_remote_copy(
                src_ref=state0.at[field, :, pl.ds(OFF + first, count), :],
                dst_ref=state0.at[field, :, pl.ds(OFF + first + shift, count), :],
                send_sem=x_send.at[field, way],
                recv_sem=x_recv.at[field, way],
                device_id=device(column + (1 if way == 0 else -1), ring, core),
                device_id_type=MESH,
            )
            copy.start()
            group.append(copy)
        if field < 2:
            for way in (0, 1):
                first, shift = (14, -32) if way == 0 else (0, 32)
                copy = pltpu.make_async_remote_copy(
                    src_ref=state0.at[field, :, pl.ds(OFF + first, 2), :],
                    dst_ref=state0.at[field, :, pl.ds(OFF + first + shift, 2), :],
                    send_sem=far_send.at[field, way],
                    recv_sem=far_recv.at[field, way],
                    device_id=device(column + (2 if way == 0 else -2), ring, core),
                    device_id_type=MESH,
                )
                copy.start()
                group.append(copy)
        x_copies.append(group)
        sends += group

    for copy in x_copies[0]:
        copy.wait_recv()

    def take_log(piece, carry):
        for block in range(7):
            at = pl.ds(OFF - 18 + SUB * block, SUB)
            logs[0, piece, at, :] = jnp.log(state0[0, piece, at, :])
        return carry

    lax.fori_loop(0, PIECES, take_log, 0)

    for field in (1, 2, 3):
        for copy in x_copies[field]:
            copy.wait_recv()

    def keep(ref, fields):
        def store(piece, row, values):
            for field, value in zip(fields, values):
                ref[field, piece, pl.ds(OFF + row, SUB), :] = value

        return store

    def keep_log(ref):
        def store(piece, row, new, thick):
            ref[0, piece, pl.ds(OFF + row, SUB), :] = new

        return store

    def keep_thick(piece, row, new, thick):
        logs[0, piece, pl.ds(OFF + row, SUB), :] = thick

    states = (state0, state1, state2)
    mass_stage(reader(logs, 0), state0, pressure, divergence, 0, -16, 6, keep_log(state1))
    stage(functools.partial(wind_piece, state0, pressure, 0), -12, 5, keep(state1, (1, 2, 3)))
    mass_stage(reader(state1, 0), state1, pressure, divergence, 1, -12, 5, keep_log(state2))
    stage(functools.partial(wind_piece, state1, pressure, 1), -8, 4, keep(state2, (1, 2, 3)))
    mass_stage(reader(state2, 0), state2, pressure, divergence, 2, -4, 3, keep_thick)

    level = owned_level(ring, core)
    lev = lax.rem(ring, 4) * 2 + core

    def give(piece, part, out, got):
        for tile_half in (0, 1):
            mine = jnp.logical_and(piece == lev, high == tile_half)
            slot = piece * 2 + tile_half

            @pl.when(mine)
            def _():
                pltpu.make_async_copy(out.at[piece, tile_half], got.at[level], own_sem.at[part]).start()

            @pl.when(jnp.logical_not(mine))
            def _():
                pltpu.make_async_remote_copy(
                    src_ref=out.at[piece, tile_half],
                    dst_ref=got.at[level],
                    send_sem=all_send.at[part, slot],
                    recv_sem=all_recv.at[part, level],
                    device_id=(column * 2 + tile_half, piece),
                    device_id_type=MESH,
                ).start()

    def last_winds(turn, carry):
        piece = lax.rem(lax.rem(ring, 4) * 2 + turn, PIECES)
        lane = lanes()
        for tile_half in (0, 1):
            row = SUB * tile_half
            out_a[piece, tile_half, 0, :, :] = logs[0, piece, pl.ds(OFF + row, SUB), :]
            for n, value in enumerate(wind_piece(state2, pressure, 2, piece, row, lane)):
                out_a[piece, tile_half, n + 1, :, :] = value
        give(piece, 0, out_a, got_a)
        return carry

    lax.fori_loop(0, PIECES, last_winds, 0)

    for field in (4, 5):
        for copy in x_copies[field]:
            copy.wait_recv()

    stage(functools.partial(passive_piece, state0, divergence, 0), -8, 4, keep(state1, (4, 5)))
    stage(functools.partial(passive_piece, state1, divergence, 1), -4, 3, keep(state2, (4, 5)))

    def last_passive(turn, carry):
        piece = lax.rem(lax.rem(ring, 4) * 2 + turn, PIECES)
        lane = lanes()
        for tile_half in (0, 1):
            for n, value in enumerate(passive_piece(state2, divergence, 2, piece, SUB * tile_half, lane)):
                out_b[piece, tile_half, n, :, :] = value
        give(piece, 1, out_b, got_b)
        return carry

    lax.fori_loop(0, PIECES, last_passive, 0)

    for copy in sends:
        copy.wait_send()

    def finish(part, out, got):
        def run(slot, carry):
            @pl.when(slot != lev * 2 + high)
            def _():
                pltpu.make_async_copy(out.at[0, 0], out.at[0, 0], all_send.at[part, slot]).wait()

            @pl.when(slot != level)
            def _():
                pltpu.make_async_copy(got.at[slot], got.at[slot], all_recv.at[part, slot]).wait()

            return carry

        lax.fori_loop(0, LEVELS, run, 0)
        pltpu.make_async_copy(out.at[0, 0], got.at[0], own_sem.at[part]).wait()

    finish(0, out_a, got_a)
    finish(1, out_b, got_b)


def advance(fields):
    state = pltpu.VMEM((FIELDS, PIECES, ROWS, LANES), jnp.float32)
    return pl.pallas_call(
        advance_kernel,
        out_shape=(
            jax.ShapeDtypeStruct((LEVELS, 4, SUB, LANES), jnp.float32),
            jax.ShapeDtypeStruct((LEVELS, 2, SUB, LANES), jnp.float32),
        ),
        in_specs=[pl.BlockSpec(memory_space=pl.ANY)] * FIELDS,
        out_specs=(pl.BlockSpec(memory_space=pl.ANY), pl.BlockSpec(memory_space=pl.ANY)),
        scratch_shapes=[
            state,
            state,
            state,
            pltpu.VMEM((1, PIECES, ROWS, LANES), jnp.float32),
            pltpu.VMEM((3, PIECES, ROWS, LANES), jnp.float32),
            pltpu.VMEM((3, PIECES, ROWS, LANES), jnp.float32),
            pltpu.VMEM((PIECES, 2, 4, SUB, LANES), jnp.float32),
            pltpu.VMEM((PIECES, 2, 2, SUB, LANES), jnp.float32),
            pltpu.SemaphoreType.DMA((FIELDS, 2)),
            pltpu.SemaphoreType.DMA((FIELDS, 2)),
            pltpu.SemaphoreType.DMA((FIELDS, 2)),
            pltpu.SemaphoreType.DMA((FIELDS, 2)),
            pltpu.SemaphoreType.DMA((2, 2)),
            pltpu.SemaphoreType.DMA((2, 2)),
            pltpu.SemaphoreType.DMA((2, LEVELS)),
            pltpu.SemaphoreType.DMA((2, LEVELS)),
            pltpu.SemaphoreType.DMA((2,)),
        ],
        name="advance",
        compiler_params=pltpu.CompilerParams(
            collective_id=0, has_side_effects=True, vmem_limit_bytes=32 * 1024 * 1024
        ),
    )(*fields)


def remap_kernel(got_a, got_b, index_ref, slot_ref, *outs):
    thick = [got_a[k, 0] for k in range(LEVELS)]
    before = [jnp.zeros_like(thick[0])]
    for k in range(LEVELS):
        before.append(before[-1] + thick[k])
    picks, parts = [], []
    mass = [before[0]]
    for j in range(1, LEVELS):
        upper = index_ref[j - 1] == j
        x = slot_ref[j - 1].astype(jnp.float32) * (1.0 / SLOTS)
        square = 0.5 * x * x
        bend = square - x * x * x * (1.0 / 3.0)
        at = jnp.where(upper, thick[j], thick[j - 1])
        mass.append(jnp.where(upper, before[j], before[j - 1]) + x * at)
        picks.append(upper)
        parts.append((at, x - square - 3.0 * bend, square - 3.0 * bend, 6.0 * bend))
    mass.append(before[LEVELS])
    layer = []
    for j in range(LEVELS):
        layer.append(mass[j + 1] - mass[j])
        outs[0][j] = layer[j]
    for field in range(5):
        if field < 3:
            f = [got_a[k, field + 1] for k in range(LEVELS)]
        else:
            f = [got_b[k, field - 3] for k in range(LEVELS)]
        edge = [f[0], 0.5 * (f[0] + f[1])]
        for k in range(2, LEVELS - 1):
            edge.append((7.0 * (f[k - 1] + f[k]) - (f[k - 2] + f[k + 1])) * (1.0 / 12.0))
        edge += [0.5 * (f[-2] + f[-1]), f[-1]]
        running = jnp.zeros_like(f[0])
        sums = [running]
        for k in range(LEVELS):
            running = running + thick[k] * f[k]
            sums.append(running)
        last = sums[0]
        for j in range(1, LEVELS + 1):
            if j < LEVELS:
                upper = picks[j - 1]
                at, w_left, w_right, w_mid = parts[j - 1]
                left = jnp.where(upper, edge[j], edge[j - 1])
                right = jnp.where(upper, edge[j + 1], edge[j])
                mid = jnp.where(upper, f[j], f[j - 1])
                base = jnp.where(upper, sums[j], sums[j - 1])
                content = base + at * (w_left * left + w_right * right + w_mid * mid)
            else:
                content = sums[LEVELS]
            outs[field + 1][j - 1] = (content - last) / layer[j - 1]
            last = content


def remap(got_a, got_b, index, slot):
    vmem = pl.BlockSpec(memory_space=pltpu.VMEM)
    return pl.pallas_call(
        remap_kernel,
        out_shape=tuple(jax.ShapeDtypeStruct((LEVELS, SUB, LANES), jnp.float32) for _ in range(6)),
        in_specs=[vmem] * 4,
        out_specs=tuple([vmem] * 6),
        name="remap",
    )(got_a, got_b, index, slot)


def body(thickness, wind_east, wind_north, theta, tracer, wind_vertical, cross_index, cross_slot):
    fields = [
        f.reshape(2, SUB, PIECES, LANES).transpose(0, 2, 1, 3)
        for f in (thickness, wind_east, wind_north, theta, tracer, wind_vertical)
    ]
    got_a, got_b = advance(fields)
    return tuple(remap(got_a, got_b, cross_index, cross_slot))


def solution(mesh):
    split = P("lev", "tile", None)
    joined = P(None, "tile", "lev")
    return jax.shard_map(
        body,
        mesh=mesh,
        in_specs=(split,) * 6 + (joined,) * 2,
        out_specs=(joined,) * 6,
        check_vma=False,
    )
```

time: 219 us -> 52.3 us (0.24)
  starting transfers between devices: 60.8 us -> 0 us
  Pallas kernels: 0 us -> 44.9 us
  other arithmetic: 42.8 us -> 0 us
  waiting for transfers between devices: 42.7 us -> 0 us
  local copies, waits for them, and re-layouts: 45.2 us -> 6.35 us
  blocking collectives: 25.2 us -> 0 us
    ppermute x12 -> x0, starting transfers between devices: 60.8 us -> none  [the longest x6 52.8 us: extended(): lax.ppermute(head, axis, [((i + 1) % count, i) for i in range(count)])]
    pallas_call x0 -> x2, Pallas kernels: none -> 44.9 us  [the longest x1 43 us: advance(): pl.pallas_call(advance_kernel, out_shape=(jax.ShapeDtypeStruct((LEVELS, 4...]
    ppermute x12 -> x0, waiting for transfers between devices: 42.7 us -> none  [the longest x6 40.8 us: extended(): lax.ppermute(tail, axis, [(i, (i + 1) % count) for i in range(count)])]
    all_to_all x1 -> x0, blocking collectives: 25.2 us -> none  [body(): lax.all_to_all(state, 'lev', split_axis=3, concat_axis=1, tiled=True)]
    unnamed x28 -> x16, local copies, waits for them, and re-layouts: 27.2 us -> 6.35 us
    mul x11 -> x0, other arithmetic: 15.1 us -> none  [the longest x3 10.5 us: advance(): damps = damping * (sixth_x(padded) + sixth_of_y)]
    add x5 -> x0, other arithmetic: 14.7 us -> none  [the longest x3 12.9 us: advance(): carried = east[None] * slope_x + north[None] * slope_y]
    slice x31 -> x0, local copies, waits for them, and re-layouts: 9.99 us -> none  [the longest x2 5.39 us: body(): columns[1]]
  transfers between devices with their start and end apart: 12 -> 0, of which waited for: 9 -> 0; matrix products, arithmetic and copies ran while one was open for 2% -> 0% of each run, Pallas kernels for 0% -> 0%
where the time goes in v1:
time: 52.3 us; the launch traced here: 51.9 us
  Pallas kernels  44.9 us (86%)
  local copies, waits for them, and re-layouts  6.35 us (12%)
  between operations  0.66 us (1%)
    pallas_call x1, Pallas kernels, advance(): pl.pallas_call(advance_kernel, out_shape=(jax.ShapeDtypeStruct((LEVELS, 4...  43 us
    unnamed x16, local copies, waits for them, and re-layouts  6.35 us
    pallas_call x1, Pallas kernels, remap(): pl.pallas_call(remap_kernel, out_shape=tuple((jax.ShapeDtypeStruct((LEVEL...  1.91 us

profile of v1, /device:TPU:1, one launch (start us, length us, event | category | flops | bytes accessed | tf_op | source)
XLA Modules:
  0.0 51.9 jit_solution(10794723104174792557)
XLA Ops:
  0.6 0.0 copy-start.2
  0.6 0.8 %copy-done.2 = f32[2,8,1024]{2,1,0:T(8,128)S(1)} copy-done((f32[2,8,1024]{2,1,0:T(8,128)S(1)}, f32[2,8,1024]{2,1,0:T(8,128)}, u32[]{:S(2)}) %copy-start.2) | copy-done | bytes 65560
  1.5 0.0 copy-start.3
  1.5 0.8 %copy-done.3 = f32[2,8,1024]{2,1,0:T(8,128)S(1)} copy-done((f32[2,8,1024]{2,1,0:T(8,128)S(1)}, f32[2,8,1024]{2,1,0:T(8,128)}, u32[]{:S(2)}) %copy-start.3) | copy-done | bytes 65560
  2.3 0.0 copy-start.4
  2.3 0.8 %copy-done.4 = f32[2,8,1024]{2,1,0:T(8,128)S(1)} copy-done((f32[2,8,1024]{2,1,0:T(8,128)S(1)}, f32[2,8,1024]{2,1,0:T(8,128)}, u32[]{:S(2)}) %copy-start.4) | copy-done | bytes 65560
  3.2 0.0 copy-start.5
  3.2 0.8 %copy-done.5 = f32[2,8,1024]{2,1,0:T(8,128)S(1)} copy-done((f32[2,8,1024]{2,1,0:T(8,128)S(1)}, f32[2,8,1024]{2,1,0:T(8,128)}, u32[]{:S(2)}) %copy-start.5) | copy-done | bytes 65560
  4.0 0.0 copy-start.6
  4.0 0.8 %copy-done.6 = f32[2,8,1024]{2,1,0:T(8,128)S(1)} copy-done((f32[2,8,1024]{2,1,0:T(8,128)S(1)}, f32[2,8,1024]{2,1,0:T(8,128)}, u32[]{:S(2)}) %copy-start.6) | copy-done | bytes 65560
  4.8 0.0 copy-start.7
  4.8 0.8 %copy-done.7 = f32[2,8,1024]{2,1,0:T(8,128)S(1)} copy-done((f32[2,8,1024]{2,1,0:T(8,128)S(1)}, f32[2,8,1024]{2,1,0:T(8,128)}, u32[]{:S(2)}) %copy-start.7) | copy-done | bytes 65560
  5.7 43.0 %advance.1 = (f32[16,4,8,128]{3,2,1,0:T(8,128)S(1)}, f32[16,2,8,128]{3,2,1,0:T(8,128)S(1)}) custom-call(f32[2,8,8,128]{3,2,1,0:T(8,128)S(1)} %bitcast.18, f32[2,8,8,128]{3,2,1,0:T(8,128)S(1)} %bitcast.19, f32[2,8,8,128]{3,2,1,0:T(8,128)S(1)} %bitcast.20, f32[2,8,8,128]{3,2,1,0:T(8,128)S(1)} %bitcast.21, f32[2,8,8,128]{3,2,1,0:T(8,128)S(1)} %bitcast.22, ...), custom_call_target="tpu_custom_call" | custom-call | tf_op jit(solution)/shard_map/advance/pallas_call | solution.py:350
  48.7 0.0 copy-start
  48.7 0.7 %copy-done = f32[16,4,8,128]{3,2,1,0:T(8,128)} copy-done((f32[16,4,8,128]{3,2,1,0:T(8,128)}, f32[16,4,8,128]{3,2,1,0:T(8,128)S(1)}, u32[]{:S(2)}) %copy-start) | copy-done | bytes 262168
  49.4 0.0 copy-start.1
  49.4 0.6 %copy-done.1 = f32[16,2,8,128]{3,2,1,0:T(8,128)} copy-done((f32[16,2,8,128]{3,2,1,0:T(8,128)}, f32[16,2,8,128]{3,2,1,0:T(8,128)S(1)}, u32[]{:S(2)}) %copy-start.1) | copy-done | bytes 131096
  50.0 1.9 %remap.1 = (f32[16,8,128]{2,1,0:T(8,128)}, f32[16,8,128]{2,1,0:T(8,128)}, f32[16,8,128]{2,1,0:T(8,128)}, f32[16,8,128]{2,1,0:T(8,128)}, f32[16,8,128]{2,1,0:T(8,128)}, /*index=5*/f32[16,8,128]{2,1,0:T(8,128)}) custom-call(f32[16,4,8,128]{3,2,1,0:T(8,128)} %copy-done, f32[16,2,8,128]{3,2,1,0:T(8,128)} %copy-done.1, s32[15,8,128]{2,1,0:T(8,128)} %index_ref.1, ...), custom_call_target="tpu_custom_call" | custom-call | tf_op jit(solution)/shard_map/remap/pallas_call | solution.py:437
Async XLA Ops:
  0.6 0.8 %copy-start.2 = (f32[2,8,1024]{2,1,0:T(8,128)S(1)}, f32[2,8,1024]{2,1,0:T(8,128)}, u32[]{:S(2)}) copy-start(f32[2,8,1024]{2,1,0:T(8,128)} %param.8) | copy-start | bytes 196612
  1.5 0.8 %copy-start.3 = (f32[2,8,1024]{2,1,0:T(8,128)S(1)}, f32[2,8,1024]{2,1,0:T(8,128)}, u32[]{:S(2)}) copy-start(f32[2,8,1024]{2,1,0:T(8,128)} %param.9) | copy-start | bytes 196612
  2.3 0.8 %copy-start.4 = (f32[2,8,1024]{2,1,0:T(8,128)S(1)}, f32[2,8,1024]{2,1,0:T(8,128)}, u32[]{:S(2)}) copy-start(f32[2,8,1024]{2,1,0:T(8,128)} %param.10) | copy-start | bytes 196612
  3.2 0.8 %copy-start.5 = (f32[2,8,1024]{2,1,0:T(8,128)S(1)}, f32[2,8,1024]{2,1,0:T(8,128)}, u32[]{:S(2)}) copy-start(f32[2,8,1024]{2,1,0:T(8,128)} %param.11) | copy-start | bytes 196612
  4.0 0.8 %copy-start.6 = (f32[2,8,1024]{2,1,0:T(8,128)S(1)}, f32[2,8,1024]{2,1,0:T(8,128)}, u32[]{:S(2)}) copy-start(f32[2,8,1024]{2,1,0:T(8,128)} %param.12) | copy-start | bytes 196612
  4.8 0.8 %copy-start.7 = (f32[2,8,1024]{2,1,0:T(8,128)S(1)}, f32[2,8,1024]{2,1,0:T(8,128)}, u32[]{:S(2)}) copy-start(f32[2,8,1024]{2,1,0:T(8,128)} %param.13) | copy-start | bytes 196612
  48.7 0.7 %copy-start = (f32[16,4,8,128]{3,2,1,0:T(8,128)}, f32[16,4,8,128]{3,2,1,0:T(8,128)S(1)}, u32[]{:S(2)}) copy-start(f32[16,4,8,128]{3,2,1,0:T(8,128)S(1)} %get-tuple-element.8.got_a) | copy-start | bytes 786436
  49.4 0.6 %copy-start.1 = (f32[16,2,8,128]{3,2,1,0:T(8,128)}, f32[16,2,8,128]{3,2,1,0:T(8,128)S(1)}, u32[]{:S(2)}) copy-start(f32[16,2,8,128]{3,2,1,0:T(8,128)S(1)} %get-tuple-element.9.got_b) | copy-start | bytes 393220

commit v2 on v1

--- a/solution.py
+++ b/solution.py
@@ -23,6 +23,7 @@
 COLUMNS = 16
 OFF = 24
 ROWS = 64
+AHEAD = 2
 
 REACH = (((0, 16), (0, 16)), ((0, 16), (0, 16)), ((1, 15), (0, 15)), ((1, 15), (0, 15)), ((7, 9), (0, 9)), ((7, 9), (0, 9)))
 
@@ -166,14 +167,15 @@
 def advance_kernel(*refs):
     inputs = refs[:FIELDS]
     got_a, got_b = refs[FIELDS : FIELDS + 2]
-    (state0, state1, state2, logs, pressure, divergence, out_a, out_b, z_send, z_recv, x_send, x_recv, far_send, far_recv, all_send, all_recv, own_sem) = refs[FIELDS + 2 :]
+    (state0, state1, state2, logs, pressure, divergence, out_a, out_b, z_send, z_recv, x_send, x_recv, far_send, far_recv, all_send, all_recv, own_sem, ready) = refs[FIELDS + 2 :]
 
     column, ring, core = place()
     high = lax.div(ring, 4)
 
     barrier = pltpu.get_barrier_semaphore()
-    partners = [device(column + d, ring, core) for d in (1, -1, 2, -2)]
-    partners += [device(column, ring + d, lax.rem(core + c, 2)) for d in (4, 3, 5, 2, 6, 1, 7, 0) for c in (0, 1) if d or c]
+    twin = device(column, ring, 1 - core)
+    partners = [device(column + d, ring, core) for d in (2, -2, 1, -1)]
+    partners += [device(column, ring + d, core) for d in (2, -2, 1, -1)] + [twin]
     for who in partners:
         pl.semaphore_signal(barrier, inc=1, device_id=who, device_id_type=MESH)
     pl.semaphore_wait(barrier, len(partners))
@@ -192,15 +194,26 @@
                 device_id=device(column, ring + hop, core),
                 device_id_type=MESH,
             )
+            pair.append(copy)
+        z_copies.append(pair)
+
+    for field in range(AHEAD):
+        for copy in z_copies[field]:
             copy.start()
-            pair.append(copy)
-            sends.append(copy)
-        z_copies.append(pair)
 
     x_copies = []
     for field in range(FIELDS):
+        if field + AHEAD < FIELDS:
+            for copy in z_copies[field]:
+                copy.wait_send()
+            for copy in z_copies[field + AHEAD]:
+                copy.start()
+        else:
+            sends += z_copies[field]
         for copy in z_copies[field]:
             copy.wait_recv()
+        if field == 0:
+            pl.semaphore_signal(ready, inc=1, device_id=twin, device_id_type=MESH)
         group = []
         for way in (0, 1):
             first, count = REACH[field][way]
@@ -269,6 +282,7 @@
     stage(functools.partial(wind_piece, state1, pressure, 1), -8, 4, keep(state2, (1, 2, 3)))
     mass_stage(reader(state2, 0), state2, pressure, divergence, 2, -4, 3, keep_thick)
 
+    pl.semaphore_wait(ready, 1)
     level = owned_level(ring, core)
     lev = lax.rem(ring, 4) * 2 + core
 
@@ -373,10 +387,11 @@
             pltpu.SemaphoreType.DMA((2, LEVELS)),
             pltpu.SemaphoreType.DMA((2, LEVELS)),
             pltpu.SemaphoreType.DMA((2,)),
+            pltpu.SemaphoreType.REGULAR,
         ],
         name="advance",
         compiler_params=pltpu.CompilerParams(
-            collective_id=0, has_side_effects=True, vmem_limit_bytes=32 * 1024 * 1024
+            collective_id=0, has_side_effects=True, vmem_limit_bytes=60 * 1024 * 1024
         ),
     )(*fields)
 

time: 52.3 us -> 44.5 us (0.85)
  local copies, waits for them, and re-layouts: 6.35 us -> 0 us
  Pallas kernels: 44.9 us -> 43.7 us
    unnamed x16 -> x0, local copies, waits for them, and re-layouts: 6.35 us -> none
    pallas_call x1, Pallas kernels: 43 us -> 41.8 us  [advance(): pl.pallas_call(advance_kernel, out_shape=(jax.ShapeDtypeStruct((LEVELS, 4...]
where the time goes in v2:
time: 44.5 us; the launch traced here: 44.4 us
  Pallas kernels  43.7 us (98%)
  between operations  0.64 us (1%)
    pallas_call x1, Pallas kernels, advance(): pl.pallas_call(advance_kernel, out_shape=(jax.ShapeDtypeStruct((LEVELS, 4...  41.8 us
    pallas_call x1, Pallas kernels, remap(): pl.pallas_call(remap_kernel, out_shape=tuple((jax.ShapeDtypeStruct((LEVEL...  1.91 us

profile of v2, /device:TPU:1, one launch (start us, length us, event | category | flops | bytes accessed | tf_op | source)
XLA Modules:
  0.0 44.4 jit_solution(7083192722031066269)
XLA Ops:
  0.6 41.8 %advance.1 = (f32[16,4,8,128]{3,2,1,0:T(8,128)}, f32[16,2,8,128]{3,2,1,0:T(8,128)}) custom-call(f32[2,8,8,128]{3,2,1,0:T(8,128)} %bitcast.18, f32[2,8,8,128]{3,2,1,0:T(8,128)} %bitcast.19, f32[2,8,8,128]{3,2,1,0:T(8,128)} %bitcast.20, f32[2,8,8,128]{3,2,1,0:T(8,128)} %bitcast.21, f32[2,8,8,128]{3,2,1,0:T(8,128)} %bitcast.22, f32[2,8,8,128]{3,2,1,0:T(8,128)} %bitcast.23), custom_call_target="tpu_custom_call" | custom-call | tf_op jit(solution)/shard_map/advance/pallas_call | solution.py:364
  42.4 1.9 %remap.1 = (f32[16,8,128]{2,1,0:T(8,128)}, f32[16,8,128]{2,1,0:T(8,128)}, f32[16,8,128]{2,1,0:T(8,128)}, f32[16,8,128]{2,1,0:T(8,128)}, f32[16,8,128]{2,1,0:T(8,128)}, /*index=5*/f32[16,8,128]{2,1,0:T(8,128)}) custom-call(f32[16,4,8,128]{3,2,1,0:T(8,128)} %get-tuple-element.8.got_a, f32[16,2,8,128]{3,2,1,0:T(8,128)} %get-tuple-element.9.got_b, ...), custom_call_target="tpu_custom_call" | custom-call | tf_op jit(solution)/shard_map/remap/pallas_call | solution.py:452

commit v3 on v2

--- a/solution.py
+++ b/solution.py
@@ -20,10 +20,12 @@
 PIECES = 8
 LEVELS = 16
 FIELDS = 6
+PARTS = 3
 COLUMNS = 16
 OFF = 24
 ROWS = 64
 AHEAD = 2
+UNROLL = 8
 
 REACH = (((0, 16), (0, 16)), ((0, 16), (0, 16)), ((1, 15), (0, 15)), ((1, 15), (0, 15)), ((7, 9), (0, 9)), ((7, 9), (0, 9)))
 
@@ -103,30 +105,33 @@
     return get
 
 
-def mass_stage(log_get, old, pressure, divergence, step, start, blocks, store):
+def mass_piece(log_get, old, pressure, divergence, step, piece, row, lane, store, with_theta):
+    east = reader(old, 1)
+    north = reader(old, 2)
+    by_x = weights(east(piece, row))
+    n_here, n_ahead, n_behind = shifted_y(north, piece, row, lane)
+    by_y = weights(n_here)
+    div = slope(*shifted_x(east, piece, row)) + slope(n_ahead, n_behind)
+    g_here, g_ahead, g_behind = shifted_y(log_get, piece, row, lane)
+    new = stencil(g_here, shifted_x(log_get, piece, row), (g_ahead, g_behind), by_x, by_y) + div
+    thick = jnp.exp(new)
+    at = pl.ds(OFF + row, SUB)
+    divergence[step, piece, at, :] = div
+    pressure[step, piece, at, :] = reader(old, 3)(piece, row) * thick if with_theta else thick
+    store(piece, row, new, thick)
+
+
+def mass_stage(log_get, old, pressure, divergence, step, start, blocks, store, with_theta=True):
     def run(piece, carry):
         lane = lanes()
         for block in range(blocks):
-            row = start + SUB * block
-            east = reader(old, 1)
-            north = reader(old, 2)
-            by_x = weights(east(piece, row))
-            n_here, n_ahead, n_behind = shifted_y(north, piece, row, lane)
-            by_y = weights(n_here)
-            div = slope(*shifted_x(east, piece, row)) + slope(n_ahead, n_behind)
-            g_here, g_ahead, g_behind = shifted_y(log_get, piece, row, lane)
-            new = stencil(g_here, shifted_x(log_get, piece, row), (g_ahead, g_behind), by_x, by_y) + div
-            thick = jnp.exp(new)
-            at = pl.ds(OFF + row, SUB)
-            divergence[step, piece, at, :] = div
-            pressure[step, piece, at, :] = reader(old, 3)(piece, row) * thick
-            store(piece, row, new, thick)
+            mass_piece(log_get, old, pressure, divergence, step, piece, start + SUB * block, lane, store, with_theta)
         return carry
 
-    lax.fori_loop(0, PIECES, run, 0)
-
-
-def wind_piece(old, pressure, step, piece, row, lane):
+    lax.fori_loop(0, PIECES, run, 0, unroll=UNROLL)
+
+
+def wind_piece(old, pressure, step, piece, row, lane, with_theta=True):
     east, north, temper, press = reader(old, 1), reader(old, 2), reader(old, 3), reader(pressure, step)
     e_here, e_ahead, e_behind = shifted_y(east, piece, row, lane)
     n_here, n_ahead, n_behind = shifted_y(north, piece, row, lane)
@@ -136,9 +141,19 @@
     new_north = stencil(n_here, shifted_x(north, piece, row), (n_ahead, n_behind), by_x, by_y)
     _, p_ahead, p_behind = shifted_y(press, piece, row, lane)
     new_north = new_north + slope(p_ahead, p_behind)
+    if not with_theta:
+        return new_east, new_north
     t_here, t_ahead, t_behind = shifted_y(temper, piece, row, lane)
     new_temper = stencil(t_here, shifted_x(temper, piece, row), (t_ahead, t_behind), by_x, by_y)
     return new_east, new_north, new_temper
+
+
+def theta_piece(old, piece, row, lane):
+    by_x = weights(reader(old, 1)(piece, row))
+    by_y = weights(reader(old, 2)(piece, row))
+    get = reader(old, 3)
+    here, ahead, behind = shifted_y(get, piece, row, lane)
+    return stencil(here, shifted_x(get, piece, row), (ahead, behind), by_x, by_y)
 
 
 def passive_piece(old, divergence, step, piece, row, lane):
@@ -161,13 +176,13 @@
             store(piece, row, body(piece, row, lane))
         return carry
 
-    lax.fori_loop(0, PIECES, run, 0)
+    lax.fori_loop(0, PIECES, run, 0, unroll=UNROLL)
 
 
 def advance_kernel(*refs):
     inputs = refs[:FIELDS]
-    got_a, got_b = refs[FIELDS : FIELDS + 2]
-    (state0, state1, state2, logs, pressure, divergence, out_a, out_b, z_send, z_recv, x_send, x_recv, far_send, far_recv, all_send, all_recv, own_sem, ready) = refs[FIELDS + 2 :]
+    got = refs[FIELDS]
+    (state0, state1, state2, logs, pressure, divergence, outgoing, z_send, z_recv, x_send, x_recv, far_send, far_recv, all_send, all_recv, own_sem, ready) = refs[FIELDS + 1 :]
 
     column, ring, core = place()
     high = lax.div(ring, 4)
@@ -202,14 +217,15 @@
             copy.start()
 
     x_copies = []
-    for field in range(FIELDS):
+
+    def pass_on(field):
         if field + AHEAD < FIELDS:
             for copy in z_copies[field]:
                 copy.wait_send()
             for copy in z_copies[field + AHEAD]:
                 copy.start()
         else:
-            sends += z_copies[field]
+            sends.extend(z_copies[field])
         for copy in z_copies[field]:
             copy.wait_recv()
         if field == 0:
@@ -242,7 +258,10 @@
                 copy.start()
                 group.append(copy)
         x_copies.append(group)
-        sends += group
+        sends.extend(group)
+
+    for field in range(4):
+        pass_on(field)
 
     for copy in x_copies[0]:
         copy.wait_recv()
@@ -253,9 +272,9 @@
             logs[0, piece, at, :] = jnp.log(state0[0, piece, at, :])
         return carry
 
-    lax.fori_loop(0, PIECES, take_log, 0)
-
-    for field in (1, 2, 3):
+    lax.fori_loop(0, PIECES, take_log, 0, unroll=UNROLL)
+
+    for field in (1, 2):
         for copy in x_copies[field]:
             copy.wait_recv()
 
@@ -275,49 +294,73 @@
     def keep_thick(piece, row, new, thick):
         logs[0, piece, pl.ds(OFF + row, SUB), :] = thick
 
-    states = (state0, state1, state2)
-    mass_stage(reader(logs, 0), state0, pressure, divergence, 0, -16, 6, keep_log(state1))
+    mass_stage(reader(logs, 0), state0, pressure, divergence, 0, -16, 6, keep_log(state1), with_theta=False)
+
+    pass_on(4)
+    pass_on(5)
+
+    for copy in x_copies[3]:
+        copy.wait_recv()
+
+    def times_theta(piece, row, lane):
+        return (pressure[0, piece, pl.ds(OFF + row, SUB), :] * reader(state0, 3)(piece, row),)
+
+    stage(times_theta, -16, 6, keep(pressure, (0,)))
     stage(functools.partial(wind_piece, state0, pressure, 0), -12, 5, keep(state1, (1, 2, 3)))
     mass_stage(reader(state1, 0), state1, pressure, divergence, 1, -12, 5, keep_log(state2))
     stage(functools.partial(wind_piece, state1, pressure, 1), -8, 4, keep(state2, (1, 2, 3)))
-    mass_stage(reader(state2, 0), state2, pressure, divergence, 2, -4, 3, keep_thick)
-
     pl.semaphore_wait(ready, 1)
     level = owned_level(ring, core)
     lev = lax.rem(ring, 4) * 2 + core
 
-    def give(piece, part, out, got):
+    def give(piece, part):
+        out = outgoing.at[part]
         for tile_half in (0, 1):
             mine = jnp.logical_and(piece == lev, high == tile_half)
             slot = piece * 2 + tile_half
 
             @pl.when(mine)
             def _():
-                pltpu.make_async_copy(out.at[piece, tile_half], got.at[level], own_sem.at[part]).start()
+                pltpu.make_async_copy(out.at[piece, tile_half], got.at[part, level], own_sem.at[part]).start()
 
             @pl.when(jnp.logical_not(mine))
             def _():
                 pltpu.make_async_remote_copy(
                     src_ref=out.at[piece, tile_half],
-                    dst_ref=got.at[level],
+                    dst_ref=got.at[part, level],
                     send_sem=all_send.at[part, slot],
                     recv_sem=all_recv.at[part, level],
                     device_id=(column * 2 + tile_half, piece),
                     device_id_type=MESH,
                 ).start()
 
+    def turned(turn):
+        return lax.rem(lax.rem(ring, 4) * 2 + turn, PIECES)
+
+    def last_mass(turn, carry):
+        piece = turned(turn)
+        lane = lanes()
+        for block in range(3):
+            mass_piece(reader(state2, 0), state2, pressure, divergence, 2, piece, -4 + SUB * block, lane, keep_thick, True)
+        for tile_half in (0, 1):
+            row = SUB * tile_half
+            outgoing[0, piece, tile_half, 0, :, :] = logs[0, piece, pl.ds(OFF + row, SUB), :]
+            outgoing[0, piece, tile_half, 1, :, :] = theta_piece(state2, piece, row, lane)
+        give(piece, 0)
+        return carry
+
+    lax.fori_loop(0, PIECES, last_mass, 0, unroll=UNROLL)
+
     def last_winds(turn, carry):
-        piece = lax.rem(lax.rem(ring, 4) * 2 + turn, PIECES)
+        piece = turned(turn)
         lane = lanes()
         for tile_half in (0, 1):
-            row = SUB * tile_half
-            out_a[piece, tile_half, 0, :, :] = logs[0, piece, pl.ds(OFF + row, SUB), :]
-            for n, value in enumerate(wind_piece(state2, pressure, 2, piece, row, lane)):
-                out_a[piece, tile_half, n + 1, :, :] = value
-        give(piece, 0, out_a, got_a)
+            for n, value in enumerate(wind_piece(state2, pressure, 2, piece, SUB * tile_half, lane, False)):
+                outgoing[1, piece, tile_half, n, :, :] = value
+        give(piece, 1)
         return carry
 
-    lax.fori_loop(0, PIECES, last_winds, 0)
+    lax.fori_loop(0, PIECES, last_winds, 0, unroll=UNROLL)
 
     for field in (4, 5):
         for copy in x_copies[field]:
@@ -327,20 +370,22 @@
     stage(functools.partial(passive_piece, state1, divergence, 1), -4, 3, keep(state2, (4, 5)))
 
     def last_passive(turn, carry):
-        piece = lax.rem(lax.rem(ring, 4) * 2 + turn, PIECES)
+        piece = turned(turn)
         lane = lanes()
         for tile_half in (0, 1):
             for n, value in enumerate(passive_piece(state2, divergence, 2, piece, SUB * tile_half, lane)):
-                out_b[piece, tile_half, n, :, :] = value
-        give(piece, 1, out_b, got_b)
+                outgoing[2, piece, tile_half, n, :, :] = value
+        give(piece, 2)
         return carry
 
-    lax.fori_loop(0, PIECES, last_passive, 0)
+    lax.fori_loop(0, PIECES, last_passive, 0, unroll=UNROLL)
 
     for copy in sends:
         copy.wait_send()
 
-    def finish(part, out, got):
+    def finish(part):
+        out = outgoing.at[part]
+
         def run(slot, carry):
             @pl.when(slot != lev * 2 + high)
             def _():
@@ -348,27 +393,24 @@
 
             @pl.when(slot != level)
             def _():
-                pltpu.make_async_copy(got.at[slot], got.at[slot], all_recv.at[part, slot]).wait()
+                pltpu.make_async_copy(got.at[part, slot], got.at[part, slot], all_recv.at[part, slot]).wait()
 
             return carry
 
         lax.fori_loop(0, LEVELS, run, 0)
-        pltpu.make_async_copy(out.at[0, 0], got.at[0], own_sem.at[part]).wait()
-
-    finish(0, out_a, got_a)
-    finish(1, out_b, got_b)
+        pltpu.make_async_copy(out.at[0, 0], got.at[part, 0], own_sem.at[part]).wait()
+
+    for part in range(PARTS):
+        finish(part)
 
 
 def advance(fields):
     state = pltpu.VMEM((FIELDS, PIECES, ROWS, LANES), jnp.float32)
     return pl.pallas_call(
         advance_kernel,
-        out_shape=(
-            jax.ShapeDtypeStruct((LEVELS, 4, SUB, LANES), jnp.float32),
-            jax.ShapeDtypeStruct((LEVELS, 2, SUB, LANES), jnp.float32),
-        ),
+        out_shape=jax.ShapeDtypeStruct((PARTS, LEVELS, 2, SUB, LANES), jnp.float32),
         in_specs=[pl.BlockSpec(memory_space=pl.ANY)] * FIELDS,
-        out_specs=(pl.BlockSpec(memory_space=pl.ANY), pl.BlockSpec(memory_space=pl.ANY)),
+        out_specs=pl.BlockSpec(memory_space=pl.ANY),
         scratch_shapes=[
             state,
             state,
@@ -376,17 +418,16 @@
             pltpu.VMEM((1, PIECES, ROWS, LANES), jnp.float32),
             pltpu.VMEM((3, PIECES, ROWS, LANES), jnp.float32),
             pltpu.VMEM((3, PIECES, ROWS, LANES), jnp.float32),
-            pltpu.VMEM((PIECES, 2, 4, SUB, LANES), jnp.float32),
-            pltpu.VMEM((PIECES, 2, 2, SUB, LANES), jnp.float32),
+            pltpu.VMEM((PARTS, PIECES, 2, 2, SUB, LANES), jnp.float32),
             pltpu.SemaphoreType.DMA((FIELDS, 2)),
             pltpu.SemaphoreType.DMA((FIELDS, 2)),
             pltpu.SemaphoreType.DMA((FIELDS, 2)),
             pltpu.SemaphoreType.DMA((FIELDS, 2)),
             pltpu.SemaphoreType.DMA((2, 2)),
             pltpu.SemaphoreType.DMA((2, 2)),
-            pltpu.SemaphoreType.DMA((2, LEVELS)),
-            pltpu.SemaphoreType.DMA((2, LEVELS)),
-            pltpu.SemaphoreType.DMA((2,)),
+            pltpu.SemaphoreType.DMA((PARTS, LEVELS)),
+            pltpu.SemaphoreType.DMA((PARTS, LEVELS)),
+            pltpu.SemaphoreType.DMA((PARTS,)),
             pltpu.SemaphoreType.REGULAR,
         ],
         name="advance",
@@ -396,8 +437,8 @@
     )(*fields)
 
 
-def remap_kernel(got_a, got_b, index_ref, slot_ref, *outs):
-    thick = [got_a[k, 0] for k in range(LEVELS)]
+def remap_kernel(got, index_ref, slot_ref, *outs):
+    thick = [got[0, k, 0] for k in range(LEVELS)]
     before = [jnp.zeros_like(thick[0])]
     for k in range(LEVELS):
         before.append(before[-1] + thick[k])
@@ -418,10 +459,8 @@
         layer.append(mass[j + 1] - mass[j])
         outs[0][j] = layer[j]
     for field in range(5):
-        if field < 3:
-            f = [got_a[k, field + 1] for k in range(LEVELS)]
-        else:
-            f = [got_b[k, field - 3] for k in range(LEVELS)]
+        part, n = ((1, 0), (1, 1), (0, 1), (2, 0), (2, 1))[field]
+        f = [got[part, k, n] for k in range(LEVELS)]
         edge = [f[0], 0.5 * (f[0] + f[1])]
         for k in range(2, LEVELS - 1):
             edge.append((7.0 * (f[k - 1] + f[k]) - (f[k - 2] + f[k + 1])) * (1.0 / 12.0))
@@ -447,15 +486,15 @@
             last = content
 
 
-def remap(got_a, got_b, index, slot):
+def remap(got, index, slot):
     vmem = pl.BlockSpec(memory_space=pltpu.VMEM)
     return pl.pallas_call(
         remap_kernel,
         out_shape=tuple(jax.ShapeDtypeStruct((LEVELS, SUB, LANES), jnp.float32) for _ in range(6)),
-        in_specs=[vmem] * 4,
+        in_specs=[vmem] * 3,
         out_specs=tuple([vmem] * 6),
         name="remap",
-    )(got_a, got_b, index, slot)
+    )(got, index, slot)
 
 
 def body(thickness, wind_east, wind_north, theta, tracer, wind_vertical, cross_index, cross_slot):
@@ -463,8 +502,7 @@
         f.reshape(2, SUB, PIECES, LANES).transpose(0, 2, 1, 3)
         for f in (thickness, wind_east, wind_north, theta, tracer, wind_vertical)
     ]
-    got_a, got_b = advance(fields)
-    return tuple(remap(got_a, got_b, cross_index, cross_slot))
+    return tuple(remap(advance(fields), cross_index, cross_slot))
 
 
 def solution(mesh):

time: 44.5 us -> 40.7 us (0.915)
  Pallas kernels: 43.7 us -> 40 us
    pallas_call x1, Pallas kernels: 41.8 us -> 38 us  [advance(): pl.pallas_call(advance_kernel, out_shape=jax.ShapeDtypeStruct((PARTS, LEV...]
where the time goes in v3:
time: 40.7 us; the launch traced here: 40.6 us
  Pallas kernels  40 us (98%)
  between operations  0.64 us (2%)
    pallas_call x1, Pallas kernels, advance(): pl.pallas_call(advance_kernel, out_shape=jax.ShapeDtypeStruct((PARTS, LEV...  38 us
    pallas_call x1, Pallas kernels, remap(): pl.pallas_call(remap_kernel, out_shape=tuple((jax.ShapeDtypeStruct((LEVEL...  1.92 us

profile of v3, /device:TPU:1, one launch (start us, length us, event | category | flops | bytes accessed | tf_op | source)
XLA Modules:
  0.0 40.6 jit_solution(5184374479016246030)
XLA Ops:
  0.6 38.0 %advance.1.got = f32[3,16,2,8,128]{4,3,2,1,0:T(8,128)} custom-call(f32[2,8,8,128]{3,2,1,0:T(8,128)} %bitcast.18, f32[2,8,8,128]{3,2,1,0:T(8,128)} %bitcast.19, f32[2,8,8,128]{3,2,1,0:T(8,128)} %bitcast.20, f32[2,8,8,128]{3,2,1,0:T(8,128)} %bitcast.21, f32[2,8,8,128]{3,2,1,0:T(8,128)} %bitcast.22, f32[2,8,8,128]{3,2,1,0:T(8,128)} %bitcast.23), custom_call_target="tpu_custom_call" | custom-call | tf_op jit(solution)/shard_map/advance/pallas_call | solution.py:409
  38.7 1.9 %remap.1 = (f32[16,8,128]{2,1,0:T(8,128)}, f32[16,8,128]{2,1,0:T(8,128)}, f32[16,8,128]{2,1,0:T(8,128)}, f32[16,8,128]{2,1,0:T(8,128)}, f32[16,8,128]{2,1,0:T(8,128)}, /*index=5*/f32[16,8,128]{2,1,0:T(8,128)}) custom-call(f32[3,16,2,8,128]{4,3,2,1,0:T(8,128)} %advance.1.got, s32[15,8,128]{2,1,0:T(8,128)} %index_ref.1, s32[15,8,128]{2,1,0:T(8,128)} %slot_ref.1), custom_call_target="tpu_custom_call" | custom-call | tf_op jit(solution)/shard_map/remap/pallas_call | solution.py:491

commit v4 on v3

--- a/solution.py
+++ b/solution.py
@@ -25,6 +25,7 @@
 OFF = 24
 ROWS = 64
 AHEAD = 2
+CUTS = 1
 UNROLL = 8
 
 REACH = (((0, 16), (0, 16)), ((0, 16), (0, 16)), ((1, 15), (0, 15)), ((1, 15), (0, 15)), ((7, 9), (0, 9)), ((7, 9), (0, 9)))
@@ -182,7 +183,7 @@
 def advance_kernel(*refs):
     inputs = refs[:FIELDS]
     got = refs[FIELDS]
-    (state0, state1, state2, logs, pressure, divergence, outgoing, z_send, z_recv, x_send, x_recv, far_send, far_recv, all_send, all_recv, own_sem, ready) = refs[FIELDS + 1 :]
+    (state0, state1, state2, logs, pressure, divergence, outgoing, z_send, z_recv, x_send, x_recv, all_send, all_recv, own_sem, ready) = refs[FIELDS + 1 :]
 
     column, ring, core = place()
     high = lax.div(ring, 4)
@@ -197,71 +198,61 @@
 
     half = pl.ds(pl.multiple_of(OFF + SUB * high, SUB), SUB)
     sends = []
+    cut = PIECES // CUTS
     z_copies = []
-    for field in range(FIELDS):
+    for n in range(FIELDS * CUTS):
+        field, span = n // CUTS, pl.ds(n % CUTS * cut, cut)
         pair = []
         for way, (level, hop) in enumerate(((high, 2), (1 - high, -2))):
-            copy = pltpu.make_async_remote_copy(
-                src_ref=inputs[field].at[level],
-                dst_ref=state0.at[field, :, half, :],
-                send_sem=z_send.at[field, way],
-                recv_sem=z_recv.at[field, way],
-                device_id=device(column, ring + hop, core),
-                device_id_type=MESH,
+            pair.append(
+                pltpu.make_async_remote_copy(
+                    src_ref=inputs[field].at[level, span],
+                    dst_ref=state0.at[field, span, half, :],
+                    send_sem=z_send.at[n, way],
+                    recv_sem=z_recv.at[n, way],
+                    device_id=device(column, ring + hop, core),
+                    device_id_type=MESH,
+                )
             )
-            pair.append(copy)
         z_copies.append(pair)
 
-    for field in range(AHEAD):
-        for copy in z_copies[field]:
+    for pair in z_copies[:AHEAD]:
+        for copy in pair:
             copy.start()
 
-    x_copies = []
-
-    def pass_on(field):
-        if field + AHEAD < FIELDS:
-            for copy in z_copies[field]:
+    x_copies = [[] for _ in range(FIELDS)]
+
+    def pass_on(n):
+        field, span = n // CUTS, pl.ds(n % CUTS * cut, cut)
+        if n + AHEAD < FIELDS * CUTS:
+            for copy in z_copies[n]:
                 copy.wait_send()
-            for copy in z_copies[field + AHEAD]:
+            for copy in z_copies[n + AHEAD]:
                 copy.start()
         else:
-            sends.extend(z_copies[field])
-        for copy in z_copies[field]:
+            sends.extend(z_copies[n])
+        for copy in z_copies[n]:
             copy.wait_recv()
-        if field == 0:
+        if n == 0:
             pl.semaphore_signal(ready, inc=1, device_id=twin, device_id_type=MESH)
-        group = []
-        for way in (0, 1):
-            first, count = REACH[field][way]
-            shift = -16 if way == 0 else 16
+        routes = [(way, hop, REACH[field][way], shift) for way, hop, shift in ((0, 1, -16), (1, -1, 16))]
+        if field < 2:
+            routes += [(2, 2, (14, 2), -32), (3, -2, (0, 2), 32)]
+        for way, hop, (first, count), shift in routes:
             copy = pltpu.make_async_remote_copy(
-                src_ref=state0.at[field, :, pl.ds(OFF + first, count), :],
-                dst_ref=state0.at[field, :, pl.ds(OFF + first + shift, count), :],
-                send_sem=x_send.at[field, way],
-                recv_sem=x_recv.at[field, way],
-                device_id=device(column + (1 if way == 0 else -1), ring, core),
+                src_ref=state0.at[field, span, pl.ds(OFF + first, count), :],
+                dst_ref=state0.at[field, span, pl.ds(OFF + first + shift, count), :],
+                send_sem=x_send.at[n, way],
+                recv_sem=x_recv.at[n, way],
+                device_id=device(column + hop, ring, core),
                 device_id_type=MESH,
             )
             copy.start()
-            group.append(copy)
-        if field < 2:
-            for way in (0, 1):
-                first, shift = (14, -32) if way == 0 else (0, 32)
-                copy = pltpu.make_async_remote_copy(
-                    src_ref=state0.at[field, :, pl.ds(OFF + first, 2), :],
-                    dst_ref=state0.at[field, :, pl.ds(OFF + first + shift, 2), :],
-                    send_sem=far_send.at[field, way],
-                    recv_sem=far_recv.at[field, way],
-                    device_id=device(column + (2 if way == 0 else -2), ring, core),
-                    device_id_type=MESH,
-                )
-                copy.start()
-                group.append(copy)
-        x_copies.append(group)
-        sends.extend(group)
-
-    for field in range(4):
-        pass_on(field)
+            x_copies[field].append(copy)
+            sends.append(copy)
+
+    for n in range(4 * CUTS):
+        pass_on(n)
 
     for copy in x_copies[0]:
         copy.wait_recv()
@@ -296,8 +287,8 @@
 
     mass_stage(reader(logs, 0), state0, pressure, divergence, 0, -16, 6, keep_log(state1), with_theta=False)
 
-    pass_on(4)
-    pass_on(5)
+    for n in range(4 * CUTS, FIELDS * CUTS):
+        pass_on(n)
 
     for copy in x_copies[3]:
         copy.wait_recv()
@@ -313,9 +304,9 @@
     level = owned_level(ring, core)
     lev = lax.rem(ring, 4) * 2 + core
 
-    def give(piece, part):
+    def give(piece, part, halves):
         out = outgoing.at[part]
-        for tile_half in (0, 1):
+        for tile_half in halves:
             mine = jnp.logical_and(piece == lev, high == tile_half)
             slot = piece * 2 + tile_half
 
@@ -334,8 +325,15 @@
                     device_id_type=MESH,
                 ).start()
 
+    def give_rest(part):
+        def run(turn, carry):
+            give(turned(turn), part, (1,))
+            return carry
+
+        lax.fori_loop(0, PIECES, run, 0)
+
     def turned(turn):
-        return lax.rem(lax.rem(ring, 4) * 2 + turn, PIECES)
+        return turn
 
     def last_mass(turn, carry):
         piece = turned(turn)
@@ -346,7 +344,7 @@
             row = SUB * tile_half
             outgoing[0, piece, tile_half, 0, :, :] = logs[0, piece, pl.ds(OFF + row, SUB), :]
             outgoing[0, piece, tile_half, 1, :, :] = theta_piece(state2, piece, row, lane)
-        give(piece, 0)
+        give(piece, 0, (0,))
         return carry
 
     lax.fori_loop(0, PIECES, last_mass, 0, unroll=UNROLL)
@@ -357,7 +355,7 @@
         for tile_half in (0, 1):
             for n, value in enumerate(wind_piece(state2, pressure, 2, piece, SUB * tile_half, lane, False)):
                 outgoing[1, piece, tile_half, n, :, :] = value
-        give(piece, 1)
+        give(piece, 1, (0,))
         return carry
 
     lax.fori_loop(0, PIECES, last_winds, 0, unroll=UNROLL)
@@ -375,33 +373,40 @@
         for tile_half in (0, 1):
             for n, value in enumerate(passive_piece(state2, divergence, 2, piece, SUB * tile_half, lane)):
                 outgoing[2, piece, tile_half, n, :, :] = value
-        give(piece, 2)
+        give(piece, 2, (0,))
         return carry
 
     lax.fori_loop(0, PIECES, last_passive, 0, unroll=UNROLL)
+    for part in range(PARTS):
+        give_rest(part)
 
     for copy in sends:
         copy.wait_send()
 
-    def finish(part):
-        out = outgoing.at[part]
-
-        def run(slot, carry):
-            @pl.when(slot != lev * 2 + high)
-            def _():
-                pltpu.make_async_copy(out.at[0, 0], out.at[0, 0], all_send.at[part, slot]).wait()
-
-            @pl.when(slot != level)
-            def _():
-                pltpu.make_async_copy(got.at[part, slot], got.at[part, slot], all_recv.at[part, slot]).wait()
-
-            return carry
-
-        lax.fori_loop(0, LEVELS, run, 0)
-        pltpu.make_async_copy(out.at[0, 0], got.at[part, 0], own_sem.at[part]).wait()
-
+    def sent(n, carry):
+        part, slot = lax.div(n, LEVELS), lax.rem(n, LEVELS)
+
+        @pl.when(slot != lev * 2 + high)
+        def _():
+            pltpu.make_async_copy(outgoing.at[0, 0, 0], outgoing.at[0, 0, 0], all_send.at[part, slot]).wait()
+
+        return carry
+
+    def arrived(n, carry):
+        part, slot = lax.div(n, LEVELS), lax.rem(n, LEVELS)
+
+        @pl.when(slot != level)
+        def _():
+            pltpu.make_async_copy(got.at[part, slot], got.at[part, slot], all_recv.at[part, slot]).wait()
+
+        return carry
+
+    lax.fori_loop(0, 2 * LEVELS, sent, 0)
     for part in range(PARTS):
-        finish(part)
+        pltpu.make_async_copy(outgoing.at[part, 0, 0], got.at[part, 0], own_sem.at[part]).wait()
+    lax.fori_loop(0, 2 * LEVELS, arrived, 0)
+    lax.fori_loop(2 * LEVELS, 3 * LEVELS, sent, 0)
+    lax.fori_loop(2 * LEVELS, 3 * LEVELS, arrived, 0)
 
 
 def advance(fields):
@@ -419,12 +424,10 @@
             pltpu.VMEM((3, PIECES, ROWS, LANES), jnp.float32),
             pltpu.VMEM((3, PIECES, ROWS, LANES), jnp.float32),
             pltpu.VMEM((PARTS, PIECES, 2, 2, SUB, LANES), jnp.float32),
-            pltpu.SemaphoreType.DMA((FIELDS, 2)),
-            pltpu.SemaphoreType.DMA((FIELDS, 2)),
-            pltpu.SemaphoreType.DMA((FIELDS, 2)),
-            pltpu.SemaphoreType.DMA((FIELDS, 2)),
-            pltpu.SemaphoreType.DMA((2, 2)),
-            pltpu.SemaphoreType.DMA((2, 2)),
+            pltpu.SemaphoreType.DMA((FIELDS * CUTS, 2)),
+            pltpu.SemaphoreType.DMA((FIELDS * CUTS, 2)),
+            pltpu.SemaphoreType.DMA((FIELDS * CUTS, 4)),
+            pltpu.SemaphoreType.DMA((FIELDS * CUTS, 4)),
             pltpu.SemaphoreType.DMA((PARTS, LEVELS)),
             pltpu.SemaphoreType.DMA((PARTS, LEVELS)),
             pltpu.SemaphoreType.DMA((PARTS,)),

time: 40.7 us -> 39.9 us (0.980)
  Pallas kernels: 40 us -> 39.1 us
    pallas_call x1, Pallas kernels: 38 us -> 37.1 us  [advance(): pl.pallas_call(advance_kernel, out_shape=jax.ShapeDtypeStruct((PARTS, LEV...]
where the time goes in v4:
time: 39.9 us; the launch traced here: 39.7 us
  Pallas kernels  39.1 us (98%)
  between operations  0.64 us (2%)
    pallas_call x1, Pallas kernels, advance(): pl.pallas_call(advance_kernel, out_shape=jax.ShapeDtypeStruct((PARTS, LEV...  37.1 us
    pallas_call x1, Pallas kernels, remap(): pl.pallas_call(remap_kernel, out_shape=tuple((jax.ShapeDtypeStruct((LEVEL...  1.92 us

profile of v4, /device:TPU:1, one launch (start us, length us, event | category | flops | bytes accessed | tf_op | source)
XLA Modules:
  0.0 39.7 jit_solution(11145131143077790065)
XLA Ops:
  0.6 37.1 %advance.1.got = f32[3,16,2,8,128]{4,3,2,1,0:T(8,128)} custom-call(f32[2,8,8,128]{3,2,1,0:T(8,128)} %bitcast.18, f32[2,8,8,128]{3,2,1,0:T(8,128)} %bitcast.19, f32[2,8,8,128]{3,2,1,0:T(8,128)} %bitcast.20, f32[2,8,8,128]{3,2,1,0:T(8,128)} %bitcast.21, f32[2,8,8,128]{3,2,1,0:T(8,128)} %bitcast.22, f32[2,8,8,128]{3,2,1,0:T(8,128)} %bitcast.23), custom_call_target="tpu_custom_call" | custom-call | tf_op jit(solution)/shard_map/advance/pallas_call | solution.py:414
  37.8 1.9 %remap.1 = (f32[16,8,128]{2,1,0:T(8,128)}, f32[16,8,128]{2,1,0:T(8,128)}, f32[16,8,128]{2,1,0:T(8,128)}, f32[16,8,128]{2,1,0:T(8,128)}, f32[16,8,128]{2,1,0:T(8,128)}, /*index=5*/f32[16,8,128]{2,1,0:T(8,128)}) custom-call(f32[3,16,2,8,128]{4,3,2,1,0:T(8,128)} %advance.1.got, s32[15,8,128]{2,1,0:T(8,128)} %index_ref.1, s32[15,8,128]{2,1,0:T(8,128)} %slot_ref.1), custom_call_target="tpu_custom_call" | custom-call | tf_op jit(solution)/shard_map/remap/pallas_call | solution.py:494

commit v5 on v4

--- a/solution.py
+++ b/solution.py
@@ -285,10 +285,10 @@
     def keep_thick(piece, row, new, thick):
         logs[0, piece, pl.ds(OFF + row, SUB), :] = thick
 
-    mass_stage(reader(logs, 0), state0, pressure, divergence, 0, -16, 6, keep_log(state1), with_theta=False)
-
     for n in range(4 * CUTS, FIELDS * CUTS):
         pass_on(n)
+
+    mass_stage(reader(logs, 0), state0, pressure, divergence, 0, -16, 6, keep_log(state1), with_theta=False)
 
     for copy in x_copies[3]:
         copy.wait_recv()

time: 39.9 us -> 39.9 us (level)
  no operation moved by 1% of the time
where the time goes in v5:
time: 39.9 us; the launch traced here: 39.7 us
  Pallas kernels  39 us (98%)
  between operations  0.64 us (2%)
    pallas_call x1, Pallas kernels, advance(): pl.pallas_call(advance_kernel, out_shape=jax.ShapeDtypeStruct((PARTS, LEV...  37.1 us
    pallas_call x1, Pallas kernels, remap(): pl.pallas_call(remap_kernel, out_shape=tuple((jax.ShapeDtypeStruct((LEVEL...  1.92 us

profile of v5, /device:TPU:1, one launch (start us, length us, event | category | flops | bytes accessed | tf_op | source)
XLA Modules:
  0.0 39.7 jit_solution(9050384997624875132)
XLA Ops:
  0.6 37.1 %advance.1.got = f32[3,16,2,8,128]{4,3,2,1,0:T(8,128)} custom-call(f32[2,8,8,128]{3,2,1,0:T(8,128)} %bitcast.18, f32[2,8,8,128]{3,2,1,0:T(8,128)} %bitcast.19, f32[2,8,8,128]{3,2,1,0:T(8,128)} %bitcast.20, f32[2,8,8,128]{3,2,1,0:T(8,128)} %bitcast.21, f32[2,8,8,128]{3,2,1,0:T(8,128)} %bitcast.22, f32[2,8,8,128]{3,2,1,0:T(8,128)} %bitcast.23), custom_call_target="tpu_custom_call" | custom-call | tf_op jit(solution)/shard_map/advance/pallas_call | solution.py:414
  37.7 1.9 %remap.1 = (f32[16,8,128]{2,1,0:T(8,128)}, f32[16,8,128]{2,1,0:T(8,128)}, f32[16,8,128]{2,1,0:T(8,128)}, f32[16,8,128]{2,1,0:T(8,128)}, f32[16,8,128]{2,1,0:T(8,128)}, /*index=5*/f32[16,8,128]{2,1,0:T(8,128)}) custom-call(f32[3,16,2,8,128]{4,3,2,1,0:T(8,128)} %advance.1.got, s32[15,8,128]{2,1,0:T(8,128)} %index_ref.1, s32[15,8,128]{2,1,0:T(8,128)} %slot_ref.1), custom_call_target="tpu_custom_call" | custom-call | tf_op jit(solution)/shard_map/remap/pallas_call | solution.py:494
